TPU v7x, 32 devices: a whole 2x2x4 slice. The times are simulated.
32 devices in a mesh: snap: 4 (over x, core), bond: 8 (over z, y).
Axes of the slice: x: 2, y: 2, z: 4, core: 2. Of those that a mesh axis runs over, the one named last changes fastest.
Arguments:
- yields: bfloat16 [4096, 32768], P('snap', 'bond'), may hold values from -60 to 60
- partners: int32 [256, 16], P('bond'), may hold values from -1 to 255, as said below
Outputs:
- bond_means: float32 [32768], P('bond')
- covariance_tiles: float32 [16, 256, 128, 128], P('snap', 'bond')
Inputs may be any that keep to these rules, and one draw needn't show every extreme that they name: `partners`: row i lists i first, then distinct blocks in ascending order among i + 1 to i + 56 - 1 (below 256), then -1 in the remaining slots; every row lists at least one block, and some row fills all 16 slots.
All inputs are finite; a program needn't handle non-finite values.
Results may differ from a plain program's by a relative error of at most 0.0007.
Values may be sent and summed in bfloat16 or wider, within the bound.
No kernel may reach another device: no remote copies, remote signals or barrier semaphores. Data moves between devices by JAX's collectives and lax.ppermute only.
A program may use at most 192 MiB of HBM per device.

v0:
```python
import jax
import jax.numpy as jnp
from jax import lax
from jax.sharding import PartitionSpec as P

BLOCK = 128
REACH = 56


def from_behind(value, axis, steps):
    count = lax.axis_size(axis)
    first, last = (max(0, -steps), min(count, count - steps))
    return lax.ppermute(value, axis, [(source, source + steps) for source in range(first, last)])


def shards(yields, partners):
    snaps_local, columns = yields.shape
    blocks_local = columns // BLOCK
    total_snaps = snaps_local * lax.axis_size("snap")
    local_sums = jnp.sum(yields, axis=0, dtype=jnp.float32)
    totals = lax.psum(local_sums, "snap")
    bond_means = totals / total_snaps
    centered = (yields.astype(jnp.float32) - bond_means[None, :]).astype(jnp.bfloat16)
    extent = blocks_local + REACH - 1
    hop_count = (extent - 1) // blocks_local
    pieces = [centered]
    for distance in range(1, hop_count + 1):
        kept_blocks = min(blocks_local, extent - distance * blocks_local)
        kept_cols = kept_blocks * BLOCK
        arrived = from_behind(centered[:, :kept_cols], "bond", -distance)
        pieces.append(arrived)
    extended = jnp.concatenate(pieces, axis=1).reshape(snaps_local, -1, BLOCK)
    ext_blocks = extended.shape[1]
    first_block = lax.axis_index("bond") * blocks_local
    live_all = partners >= 0
    index_all = jnp.clip(jnp.where(live_all, partners - first_block, 0), 0, ext_blocks - 1)
    inverse = 1.0 / (total_snaps - 1)

    def block_tiles(args):
        block_row, index_row, live_row = args
        own_block = lax.dynamic_index_in_dim(extended, block_row, 1, keepdims=False)
        chosen = jnp.take(extended, index_row, axis=1)
        tile_sum = jnp.einsum("sa,scb->cab", own_block, chosen, preferred_element_type=jnp.float32)
        return tile_sum * (live_row.astype(jnp.float32) * inverse)[:, None, None]

    per_block = lax.map(
        block_tiles, (jnp.arange(blocks_local, dtype=jnp.int32), index_all, live_all)
    )
    covariance_tiles = lax.psum_scatter(
        jnp.transpose(per_block, (1, 0, 2, 3)), "snap", scatter_dimension=0, tiled=True
    )
    return (bond_means, covariance_tiles)


def solution(mesh):
    return jax.shard_map(
        shards,
        mesh=mesh,
        in_specs=(P("snap", "bond"), P("bond", None)),
        out_specs=(P("bond"), P("snap", "bond", None, None)),
        check_vma=False,
    )
```

profile of v0, /device:TPU:24, one launch (start us, length us, event | category | flops | bytes accessed | tf_op | source)
XLA Modules:
  0.0 1245.5 jit_solution(13524217388700931612)
XLA Ops:
  7.2 11.9 copy.9
  19.2 4.6 convert_reduce_fusion
  23.7 11.2 psum.7
  34.9 8.2 fusion.17
  46.4 5.9 slice.6
  52.3 5.0 collective-permute-start.1
  57.4 296.8 %collective-permute-done.1 = bf16[1024,2944]{0,1:T(8,128)(2,1)} collective-permute-done((bf16[1024,2944]{0,1:T(8,128)(2,1)}, bf16[1024,2944]{0,1:T(8,128)(2,1)}, u32[]{:S(2)}, u32[]{:S(2)}) %collective-permute-start.1) | collective-permute-done | bytes 6029344 | tf_op jit(solution)/shard_map/ppermute | solution.py:13
  354.2 28.6 %pad_maximum_fusion = bf16[1024,11136]{0,1:T(8,128)(2,1)} fusion(bf16[1024,2944]{0,1:T(8,128)(2,1)} %collective-permute-done.1, bf16[1024,4096]{0,1:T(8,128)(2,1)} %collective-permute-done, bf16[1024,4096]{0,1:T(8,128)(2,1)} %fusion.17), kind=kLoop, calls=%fused_computation.21 | loop fusion | flops 68419584 | bytes 45613056 | tf_op jit(solution)/shard_map/concatenate | solution.py:32
  382.8 30.3 %copy.12 = bf16[1024,87,128]{2,0,1:T(8,128)(2,1)} copy(bf16[1024,87,128]{0,2,1:T(8,128)(2,1)} %bitcast.42) | data formatting | bytes 45613056 | tf_op jit(solution)/shard_map/while | solution.py:46
  413.1 589.5 %while.10 = (s32[]{:T(128)}, f32[32,16,128,128]{3,2,0,1:T(8,128)}, s32[32,16]{1,0:T(8,128)S(1)}, bf16[1024,87,128]{2,0,1:T(8,128)(2,1)}, s32[32]{0:T(128)S(1)}, ...) while((s32[]{:T(128)}, f32[32,16,128,128]{3,2,0,1:T(8,128)}, s32[32,16]{1,0:T(8,128)S(1)}, ...), condition=%wide.region_3.4_spmd, body=%wide.region_2.3_spmd.sunk | while | flops 539231424 | bytes 18093196 | solution.py:46
  415.6 10.6 gather_fusion
  426.3 3.9 fusion.27
  434.1 10.6 gather_fusion
  444.7 3.9 fusion.27
  452.5 10.6 gather_fusion
  470.9 10.6 gather_fusion
  481.6 3.9 fusion.27
  489.4 10.6 gather_fusion
  500.0 3.9 fusion.27
  507.8 10.6 gather_fusion
  526.2 10.6 gather_fusion
  536.8 3.9 fusion.27
  544.6 10.6 gather_fusion
  555.3 3.9 fusion.27
  563.0 10.6 gather_fusion
  581.4 10.6 gather_fusion
  592.1 3.9 fusion.27
  599.9 10.6 gather_fusion
  610.5 3.9 fusion.27
  618.3 10.6 gather_fusion
  628.9 3.9 fusion.27
  636.7 10.6 gather_fusion
  655.1 10.6 gather_fusion
  665.7 3.9 fusion.27
  673.5 10.6 gather_fusion
  684.1 3.9 fusion.27
  691.9 10.6 gather_fusion
  710.4 10.6 gather_fusion
  721.0 3.9 fusion.27
  728.8 10.6 gather_fusion
  747.2 10.6 gather_fusion
  765.6 10.6 gather_fusion
  784.0 10.6 gather_fusion
  794.7 3.9 fusion.27
  802.5 10.6 gather_fusion
  813.1 3.9 fusion.27
  820.9 10.6 gather_fusion
  831.5 3.9 fusion.27
  839.3 10.6 gather_fusion
  849.9 3.9 fusion.27
  857.7 10.6 gather_fusion
  868.3 3.9 fusion.27
  876.1 10.6 gather_fusion
  886.7 3.9 fusion.27
  894.5 10.6 gather_fusion
  905.2 3.9 fusion.27
  913.0 10.6 gather_fusion
  923.6 3.9 fusion.27
  931.4 10.6 gather_fusion
  949.9 10.6 gather_fusion
  968.3 10.6 gather_fusion
  978.9 3.9 fusion.27
  986.7 10.6 gather_fusion
  1002.6 236.1 %reduce-scatter.2.cloned.1.call-done = f32[4,32,128,128]{3,2,1,0:T(8,128)} async-done(((f32[16,32,128,128]{3,2,1,0:T(8,128)}), f32[4,32,128,128]{3,2,1,0:T(8,128)}) %reduce-scatter.2.cloned.1.call-update) | async-done | bytes 8388624 | tf_op jit(solution)/shard_map/reduce_scatter | solution.py:49
  (249 shorter events, 109.6 us)
Async XLA Ops:
  7.2 1231.5 %reduce-scatter.2.cloned.1.call-start = ((), (), s32[]{:S(2)}) async-start(), calls=%async_computation.1 | async-start | bytes 41943040 | tf_op jit(solution)/shard_map/reduce_scatter | solution.py:49
  19.2 38.2 %copy-start.1 = (s32[32,16]{0,1:T(8,128)S(1)}, s32[32,16]{0,1:T(8,128)}, u32[]{:S(2)}) copy-start(s32[32,16]{0,1:T(8,128)} %param.5) | copy-start | bytes 6148
  34.9 347.9 %copy-start = (f32[4096]{0:T(1024)}, f32[4096]{0:T(1024)S(1)}, u32[]{:S(2)}) copy-start(f32[4096]{0:T(1024)S(1)} %broadcast_multiply_fusion) | copy-start | bytes 49156
  43.1 311.1 %collective-permute-start = (bf16[1024,4096]{0,1:T(8,128)(2,1)}, bf16[1024,4096]{0,1:T(8,128)(2,1)}, u32[]{:S(2)}, u32[]{:S(2)}) collective-permute-start(bf16[1024,4096]{0,1:T(8,128)(2,1)} %fusion.17), channel_id=1, source_target_pairs={{1,0},{2,1},{3,2},{4,3},{5,4},{6,5},{7,6},{9,8},{10,9},{11,10},{12... | collective-permute-start | bytes 25165832 | tf_op jit(solution)/shard_map/ppermute | solution.py:13
  52.3 301.8 %collective-permute-start.1 = (bf16[1024,2944]{0,1:T(8,128)(2,1)}, bf16[1024,2944]{0,1:T(8,128)(2,1)}, u32[]{:S(2)}, u32[]{:S(2)}) collective-permute-start(bf16[1024,2944]{0,1:T(8,128)(2,1)} %slice.6), channel_id=1, source_target_pairs={{2,0},{3,1},{4,2},{5,3},{6,4},{7,5},{10,8},{11,9},{12,10},{13,11},... | collective-permute-start | bytes 18087944 | tf_op jit(solution)/shard_map/ppermute | solution.py:13
Sparse Core Ops, SparseCore 0:
  1002.7 235.8 reduce-scatter.1
where the time goes:
time: 1250 us
  waiting for transfers between devices  533 us (43%)
  local copies, waits for them, and re-layouts  449 us (36%)
  matrix products  124 us (10%)
  loops' own time  63.4 us (5%)
  other arithmetic  42.8 us (3%)
  between operations  14.1 us (1%)
    gather x32, local copies, waits for them, and re-layouts, block_tiles(): chosen = jnp.take(extended, index_row, axis=1)  339 us
    ppermute x2, waiting for transfers between devices, from_behind(): lax.ppermute(value, axis, [(source, source + steps) for source in range(f...  297 us
    reduce_scatter x1, waiting for transfers between devices, shards(): lax.psum_scatter(jnp.transpose(per_block, (1, 0, 2, 3)), 'snap', scatter_...  236 us
    dot_general x32, matrix products, block_tiles(): jnp.einsum('sa,scb->cab', own_block, chosen, preferred_element_type=jnp.f...  124 us
    another operation x1, loops' own time, shards(): lax.map(block_tiles, (jnp.arange(blocks_local, dtype=jnp.int32), index_al...  63.4 us
    dynamic_update_slice x64, local copies, waits for them, and re-layouts, shards(): lax.map(block_tiles, (jnp.arange(blocks_local, dtype=jnp.int32), index_al...  43.5 us
    while x1, local copies, waits for them, and re-layouts, shards(): lax.map(block_tiles, (jnp.arange(blocks_local, dtype=jnp.int32), index_al...  30.3 us
    concatenate x1, other arithmetic, shards(): extended = jnp.concatenate(pieces, axis=1).reshape(snaps_local, -1, BLOCK)  28.6 us
  transfers between devices with their start and end apart: 3, of which 2 were waited for; matrix products, arithmetic and copies ran while one was open for 0% of the time, Pallas kernels for 0%

commit v1 on v0

v1 whole, which is shorter than its diff:
```python
import functools

import jax
import jax.numpy as jnp
from jax import lax
from jax.experimental import pallas as pl
from jax.experimental.pallas import tpu as pltpu
from jax.sharding import PartitionSpec as P

BLOCK = 128
REACH = 56
CHUNK = 4
WINDOW = 16
UNROLL = 4
CODED = BLOCK + 8
TOP = 10.0
F32 = jnp.float32
BF16 = jnp.bfloat16
ANY = pl.BlockSpec(memory_space=pl.ANY)
SMEM = pl.BlockSpec(memory_space=pltpu.SMEM)
VMEM = pl.BlockSpec(memory_space=pltpu.VMEM)


def params(mib):
    return pltpu.CompilerParams(vmem_limit_bytes=mib << 20)


def from_behind(value, axis, steps):
    count = lax.axis_size(axis)
    first, last = (max(0, -steps), min(count, count - steps))
    return lax.ppermute(value, axis, [(source, source + steps) for source in range(first, last)])


def plain_shards(yields, partners):
    snaps_local, columns = yields.shape
    blocks_local = columns // BLOCK
    total_snaps = snaps_local * lax.axis_size("snap")
    local_sums = jnp.sum(yields, axis=0, dtype=F32)
    totals = lax.psum(local_sums, "snap")
    bond_means = totals / total_snaps
    centered = (yields.astype(F32) - bond_means[None, :]).astype(BF16)
    extent = blocks_local + REACH - 1
    hop_count = (extent - 1) // blocks_local
    pieces = [centered]
    for distance in range(1, hop_count + 1):
        kept_blocks = min(blocks_local, extent - distance * blocks_local)
        kept_cols = kept_blocks * BLOCK
        pieces.append(from_behind(centered[:, :kept_cols], "bond", -distance))
    extended = jnp.concatenate(pieces, axis=1).reshape(snaps_local, -1, BLOCK)
    ext_blocks = extended.shape[1]
    first_block = lax.axis_index("bond") * blocks_local
    live_all = partners >= 0
    index_all = jnp.clip(jnp.where(live_all, partners - first_block, 0), 0, ext_blocks - 1)
    inverse = 1.0 / (total_snaps - 1)

    def block_tiles(args):
        block_row, index_row, live_row = args
        own_block = lax.dynamic_index_in_dim(extended, block_row, 1, keepdims=False)
        chosen = jnp.take(extended, index_row, axis=1)
        tile_sum = jnp.einsum("sa,scb->cab", own_block, chosen, preferred_element_type=F32)
        return tile_sum * (live_row.astype(F32) * inverse)[:, None, None]

    per_block = lax.map(
        block_tiles, (jnp.arange(blocks_local, dtype=jnp.int32), index_all, live_all)
    )
    covariance_tiles = lax.psum_scatter(
        jnp.transpose(per_block, (1, 0, 2, 3)), "snap", scatter_dimension=0, tiled=True
    )
    return (bond_means, covariance_tiles)


def token():
    return jax.ShapeDtypeStruct((8, BLOCK), F32)


def feed_kernel(cfg, plan, info, yields, far, *refs):
    outs = refs[-4 - len(plan):-4]
    buffer, in_sems, out_sems = refs[-3:]
    wide = cfg["chunk"] * BLOCK
    rows = buffer.shape[2]
    odd = info[0]
    pieces = [(n, r) for r in range(buffer.shape[1]) for n in range(len(plan))]

    def fetch(src, cols, n, r):
        part = src.at[pl.ds(r * rows, rows), cols]
        return pltpu.make_async_copy(part, buffer.at[n, r], in_sems.at[n, r])

    def own(n, r):
        return fetch(yields, pl.ds(plan[n][1] * wide, wide), n, r)

    def relayed(n, r):
        return fetch(far, pl.ds(0, wide), n, r)

    def store(n, r):
        part = outs[n].at[pl.ds(r * rows, rows)]
        return pltpu.make_async_copy(buffer.at[n, r], part, out_sems.at[n, r])

    for n, r in pieces:
        kind = plan[n][0]
        if kind == "own":
            own(n, r).start()
        elif kind == "relay":
            relayed(n, r).start()
        else:
            pl.when(odd == 1)(lambda: own(n, r).start())
            pl.when(odd == 0)(lambda: relayed(n, r).start())
    for n, r in pieces:
        relayed(n, r).wait()
        store(n, r).start()
    for n, r in pieces:
        store(n, r).wait()


def feed(cfg, plan, odd, yields, far, *tokens):
    shape = (yields.shape[0], cfg["chunk"] * BLOCK)
    pieces = 4
    return pl.pallas_call(
        functools.partial(feed_kernel, cfg, plan),
        in_specs=[SMEM] + [ANY] * (2 + len(tokens)),
        out_specs=[ANY] * (len(plan) + 1),
        out_shape=[jax.ShapeDtypeStruct(shape, BF16)] * len(plan) + [token()],
        scratch_shapes=[
            pltpu.VMEM((len(plan), pieces, shape[0] // pieces, shape[1]), BF16),
            pltpu.SemaphoreType.DMA((len(plan), pieces)),
            pltpu.SemaphoreType.DMA((len(plan), pieces)),
        ],
        compiler_params=params(16),
        cost_estimate=pl.CostEstimate(flops=0, bytes_accessed=1 << 12, transcendentals=0),
        name="feed",
    )(odd, yields, far, *tokens)


def sums_kernel(raw_ref, _, out_ref):
    out_ref[0] = jnp.sum(raw_ref[...].astype(F32), axis=0, keepdims=True)


def column_sums(yields, after):
    snaps, columns = yields.shape
    wide = 4 * BLOCK
    steps = columns // wide
    return pl.pallas_call(
        sums_kernel,
        grid=(steps,),
        in_specs=[pl.BlockSpec((snaps, wide), lambda i: (0, i)), ANY],
        out_specs=pl.BlockSpec((1, 1, wide), lambda i: (i, 0, 0)),
        out_shape=jax.ShapeDtypeStruct((steps, 1, wide), F32),
        compiler_params=params(16),
        cost_estimate=pl.CostEstimate(flops=0, bytes_accessed=1 << 12, transcendentals=0),
        name="column_sums",
    )(yields, after).reshape(columns)


def transpose_kernel(group, raw_ref, mean_ref, out_ref):
    for g in range(group):
        cols = pl.ds(g * BLOCK, BLOCK)
        block = raw_ref[:, cols].astype(F32) - mean_ref[0, :, cols]
        out_ref[g] = block.T.astype(BF16)


def centered_transposed(yields, means):
    snaps, columns = yields.shape
    group = 2
    blocks = columns // BLOCK
    steps = blocks // group
    return pl.pallas_call(
        functools.partial(transpose_kernel, group),
        grid=(steps,),
        in_specs=[
            pl.BlockSpec((snaps, group * BLOCK), lambda i: (0, i)),
            pl.BlockSpec((1, 1, group * BLOCK), lambda i: (i, 0, 0)),
        ],
        out_specs=pl.BlockSpec((group, BLOCK, snaps), lambda i: (i, 0, 0)),
        out_shape=jax.ShapeDtypeStruct((blocks, BLOCK, snaps), BF16),
        compiler_params=params(24),
        cost_estimate=pl.CostEstimate(flops=0, bytes_accessed=1 << 12, transcendentals=0),
        name="center_transpose",
    )(yields, means.reshape(steps, 1, group * BLOCK))


def tile_loop(lo, hi, load, product, put, store):
    count = hi - lo
    groups = lax.div(count + UNROLL - 1, UNROLL)

    def start_loads(g, half):
        for u in range(UNROLL):
            for copy in load(lo + g * UNROLL + u, half * UNROLL + u):
                copy.start()

    pl.when(groups > 0)(lambda: start_loads(0, 0))

    def body(g, carry):
        half = lax.rem(g, 2)
        base = lo + g * UNROLL
        pl.when(g + 1 < groups)(lambda: start_loads(g + 1, 1 - half))
        for u in range(UNROLL):
            for copy in load(base + u, half * UNROLL + u):
                copy.wait()

        @pl.when(g >= 2)
        def _():
            for u in range(UNROLL):
                store(base + u, half * UNROLL + u).wait()

        values = [product(base + u, half * UNROLL + u) for u in range(UNROLL)]
        for u in range(UNROLL):
            put(half * UNROLL + u, values[u])
        for u in range(UNROLL):
            pl.when(base + u < hi)(lambda: store(base + u, half * UNROLL + u).start())
        return carry

    lax.fori_loop(0, groups, body, 0)

    @pl.when(groups >= 2)
    def _():
        for u in range(UNROLL):
            store(lo, lax.rem(groups, 2) * UNROLL + u).wait()

    @pl.when(groups >= 1)
    def _():
        last = groups - 1
        for u in range(UNROLL):
            pl.when(lo + last * UNROLL + u < hi)(
                lambda: store(lo, lax.rem(last, 2) * UNROLL + u).wait()
            )


def output_place(slots, mlist, out, n):
    v = mlist[n] >> 8
    return out.at[lax.rem(v, slots), lax.div(v, slots)]


def putters(cfg, mlist, out, send, stage, store_sem):
    slots = cfg["slots"]

    def put_out(slot, values):
        stage[slot, 0:BLOCK] = values

    def store_out(n, slot):
        dst = output_place(slots, mlist, out, n)
        return pltpu.make_async_copy(stage.at[slot, pl.ds(0, BLOCK)], dst, store_sem.at[slot])

    def put_send(slot, values):
        top = jnp.maximum(jnp.max(jnp.abs(values), axis=0, keepdims=True), 1e-30)
        power = TOP - jnp.ceil(jnp.log2(top))
        stage[slot, 0:BLOCK] = values * jnp.exp2(power)
        stage[slot, BLOCK:CODED] = jnp.broadcast_to(power, (CODED - BLOCK, BLOCK))

    def store_send(n, slot):
        return pltpu.make_async_copy(stage.at[slot], send.at[n], store_sem.at[slot])

    return put_out, store_out, put_send, store_send


def send_window(info, at, size, send, window, sem):
    copy = pltpu.make_async_copy(send.at[pl.ds(info[at], size)], window, sem)
    copy.start()
    copy.wait()


def own_kernel(
    cfg, info, mlist, olist, xa, xb, _, out, send, window, tok, stage, zero, store_sem, zero_sem,
    win_sem,
):
    slots, inverse = cfg["slots"], cfg["inverse"]
    blocks = xa.shape[0]

    def product(ref):
        def tile(n, slot):
            v = ref[n]
            i = lax.div(v >> 8, slots)
            p = jnp.minimum(v & 255, blocks - 1)
            dims = (((1,), (1,)), ((), ()))
            acc = lax.dot_general(xa[i], xa[p], dims, preferred_element_type=F32)
            acc += lax.dot_general(xb[i], xb[p], dims, preferred_element_type=F32)
            return acc * inverse

        return tile

    def nothing(n, slot):
        return ()

    put_out, store_out, put_send, store_send = putters(cfg, mlist, out, send, stage, store_sem)
    o_lo, m_lo = info[cfg["cut_o"]], info[cfg["cut_m"]]
    o_hi, m_hi = info[cfg["cut_o"] + 1], info[cfg["cut_m"] + 1]
    tile_loop(o_lo, o_hi, nothing, product(olist), put_send, store_send)
    tile_loop(m_lo, m_hi, nothing, product(mlist), put_out, store_out)

    zero[...] = jnp.zeros_like(zero)
    live = info[cfg["cut_m"] + cfg["stages"]]

    def clear(n):
        return pltpu.make_async_copy(zero, output_place(slots, mlist, out, n), zero_sem)

    def start_clear(n, carry):
        clear(n).start()
        return carry

    def wait_clear(n, carry):
        clear(n).wait()
        return carry

    lax.fori_loop(live, slots * blocks, start_clear, 0)
    lax.fori_loop(live, slots * blocks, wait_clear, 0)
    send_window(info, cfg["win_o"], cfg["window"], send, window, win_sem)


def own_stage(cfg, info, mlist, olist, xa, xb, after):
    blocks = xa.shape[0]
    slots, size = cfg["slots"], cfg["window"]
    return pl.pallas_call(
        functools.partial(own_kernel, cfg),
        in_specs=[SMEM, SMEM, SMEM, VMEM, VMEM, ANY],
        out_specs=[ANY] * 4,
        out_shape=[
            jax.ShapeDtypeStruct((slots, blocks, BLOCK, BLOCK), F32),
            jax.ShapeDtypeStruct((slots * blocks + size, CODED, BLOCK), F32),
            jax.ShapeDtypeStruct((size, CODED, BLOCK), F32),
            token(),
        ],
        scratch_shapes=[
            pltpu.VMEM((2 * UNROLL, CODED, BLOCK), F32),
            pltpu.VMEM((BLOCK, BLOCK), F32),
            pltpu.SemaphoreType.DMA((2 * UNROLL,)),
            pltpu.SemaphoreType.DMA,
            pltpu.SemaphoreType.DMA,
        ],
        compiler_params=params(40),
        cost_estimate=pl.CostEstimate(flops=0, bytes_accessed=1 << 16, transcendentals=0),
        name="own_tiles",
    )(info, mlist, olist, xa, xb, after)


def merge_parts(cfg, lo, count, mlist, arrived, out, mine, theirs, mine_sem, theirs_sem):
    slots = cfg["slots"]

    def read_mine(r):
        src = output_place(slots, mlist, out, lo + r)
        return pltpu.make_async_copy(src, mine.at[r], mine_sem.at[r])

    def read_theirs(r):
        return pltpu.make_async_copy(arrived.at[r], theirs.at[r], theirs_sem.at[r])

    def write(r):
        dst = output_place(slots, mlist, out, lo + r)
        return pltpu.make_async_copy(mine.at[r], dst, mine_sem.at[r])

    def first(r, carry):
        read_mine(r).start()
        read_theirs(r).start()
        return carry

    def second(r, carry):
        read_mine(r).wait()
        read_theirs(r).wait()
        scale = jnp.exp2(-theirs[r, BLOCK:BLOCK + 1])
        mine[r] = mine[r] + theirs[r, 0:BLOCK] * scale
        write(r).start()
        return carry

    def third(r, carry):
        write(r).wait()
        return carry

    return tuple(
        lambda step=step: lax.fori_loop(0, count, step, 0) for step in (first, second, third)
    )


def merge_scratch(size):
    return [
        pltpu.VMEM((size, BLOCK, BLOCK), F32),
        pltpu.VMEM((size, CODED, BLOCK), F32),
        pltpu.SemaphoreType.DMA((size,)),
        pltpu.SemaphoreType.DMA((size,)),
    ]


def halo_kernel(cfg, hop, has_far, has_merge, *refs):
    info, mlist, olist, near_mean, far_mean, xa, xb = refs[:7]
    chunk, slots, blocks, inverse = cfg["chunk"], cfg["slots"], cfg["blocks"], cfg["inverse"]
    raw = refs[7:11] if has_far else refs[7:9]
    rest = refs[7 + len(raw):]
    if has_merge:
        arrived, rest = rest[0], rest[1:]
    _, _, _, out, send, window, _ = rest[:7]
    rawbuf, ya, yb, lhs_a, lhs_b, stage, raw_sem, lhs_sem, store_sem, win_sem = rest[7:17]
    step = hop + 1
    o_lo, o_hi = info[cfg["cut_o"] + step], info[cfg["cut_o"] + step + 1]
    m_lo, m_hi = info[cfg["cut_m"] + step], info[cfg["cut_m"] + step + 1]
    near_first = (hop - info[cfg["odd"]]) * chunk
    far_first = hop * chunk
    if has_merge:
        lo = info[cfg["win_m"] + step - 2]
        count = info[cfg["win_m"] + step - 1] - lo
        first, second, third = merge_parts(cfg, lo, count, mlist, arrived, out, *rest[17:])
        first()

    @pl.when(o_hi - o_lo + m_hi - m_lo > 0)
    def _():
        copies = [
            pltpu.make_async_copy(ref, rawbuf.at[n], raw_sem.at[n]) for n, ref in enumerate(raw)
        ]
        for copy in copies:
            copy.start()
        for n, copy in enumerate(copies):
            copy.wait()
            kind, half = n // 2, n % 2
            dst = (ya, yb)[half]
            for j in range(chunk):
                if kind == 0:
                    row = jnp.clip(near_first + j, 0, blocks - 1)
                    mean = near_mean[pl.ds(row, 1), :]
                else:
                    mean = far_mean[pl.ds(far_first + j, 1), :]
                block = rawbuf[n, :, pl.ds(j * BLOCK, BLOCK)].astype(F32) - mean
                dst[kind * chunk + j] = block.astype(BF16)

    def load(ref):
        def copies(n, slot):
            i = lax.div(ref[n] >> 8, slots)
            return (
                pltpu.make_async_copy(xa.at[i], lhs_a.at[slot], lhs_sem.at[slot, 0]),
                pltpu.make_async_copy(xb.at[i], lhs_b.at[slot], lhs_sem.at[slot, 1]),
            )

        return copies

    def product(ref):
        def tile(n, slot):
            rel = ref[n] & 255
            near = rel - blocks - near_first
            far = rel - 2 * blocks - far_first + chunk
            j = jnp.clip(jnp.where(rel >= 2 * blocks, far, near), 0, 2 * chunk - 1)
            acc = jnp.dot(lhs_a[slot], ya[j], preferred_element_type=F32)
            acc += jnp.dot(lhs_b[slot], yb[j], preferred_element_type=F32)
            return acc * inverse

        return tile

    put_out, store_out, put_send, store_send = putters(cfg, mlist, out, send, stage, store_sem)
    tile_loop(o_lo, o_hi, load(olist), product(olist), put_send, store_send)
    tile_loop(m_lo, m_hi, load(mlist), product(mlist), put_out, store_out)
    if has_merge:
        second()
    send_window(info, cfg["win_o"] + step, cfg["window"], send, window, win_sem)
    if has_merge:
        third()


def halo_stage(
    cfg, hop, info, mlist, olist, near_mean, far_mean, xa, xb, raw, arrived, out, send, after
):
    snaps = xa.shape[2]
    chunk, size = cfg["chunk"], cfg["window"]
    has_far, has_merge = len(raw) == 4, arrived is not None
    extra = [arrived] if has_merge else []
    count = 7 + len(raw) + len(extra)
    return pl.pallas_call(
        functools.partial(halo_kernel, cfg, hop, has_far, has_merge),
        in_specs=[SMEM, SMEM, SMEM, VMEM, VMEM] + [ANY] * (count - 2),
        out_specs=[ANY] * 4,
        out_shape=[
            jax.ShapeDtypeStruct(out.shape, F32),
            jax.ShapeDtypeStruct(send.shape, F32),
            jax.ShapeDtypeStruct((size, CODED, BLOCK), F32),
            token(),
        ],
        scratch_shapes=[
            pltpu.VMEM((4, snaps, chunk * BLOCK), BF16),
            pltpu.VMEM((2 * chunk, snaps, BLOCK), BF16),
            pltpu.VMEM((2 * chunk, snaps, BLOCK), BF16),
            pltpu.VMEM((2 * UNROLL, BLOCK, snaps), BF16),
            pltpu.VMEM((2 * UNROLL, BLOCK, snaps), BF16),
            pltpu.VMEM((2 * UNROLL, CODED, BLOCK), F32),
            pltpu.SemaphoreType.DMA((4,)),
            pltpu.SemaphoreType.DMA((2 * UNROLL, 2)),
            pltpu.SemaphoreType.DMA((2 * UNROLL,)),
            pltpu.SemaphoreType.DMA,
        ] + (merge_scratch(size) if has_merge else []),
        input_output_aliases={count: 0, count + 1: 1},
        compiler_params=params(32),
        cost_estimate=pl.CostEstimate(flops=0, bytes_accessed=1 << 16, transcendentals=0),
        name="halo_tiles",
    )(info, mlist, olist, near_mean, far_mean, xa, xb, *raw, *extra, out, send, after)


def merge_kernel(cfg, span, mlist, arrived, _, out, *scratch):
    lo = span[0]
    for part in merge_parts(cfg, lo, span[1] - lo, mlist, arrived, out, *scratch):
        part()


def merge(cfg, span, mlist, arrived, out):
    return pl.pallas_call(
        functools.partial(merge_kernel, cfg),
        in_specs=[SMEM, SMEM, ANY, ANY],
        out_specs=ANY,
        out_shape=jax.ShapeDtypeStruct(out.shape, F32),
        scratch_shapes=merge_scratch(cfg["window"]),
        input_output_aliases={3: 0},
        compiler_params=params(8),
        cost_estimate=pl.CostEstimate(flops=0, bytes_accessed=1 << 14, transcendentals=0),
        name="merge_tiles",
    )(span, mlist, arrived, out)


def work_list(rel, live, stage, stages):
    entries = rel.size
    ids = jnp.arange(entries, dtype=jnp.int32)
    key = jnp.where(live, stage, stages).reshape(-1) * entries + ids
    value = ids * 256 + jnp.where(live, rel, 0).reshape(-1)
    rank = jnp.sum((key[None, :] < key[:, None]).astype(jnp.int32), axis=1)
    ordered = jnp.sum(jnp.where(rank[None, :] == ids[:, None], value[None, :], 0), axis=1)
    bounds = jnp.arange(stages + 1, dtype=jnp.int32) * entries
    cuts = jnp.sum((key[None, :] < bounds[:, None]).astype(jnp.int32), axis=1)
    padded = jnp.pad(ordered.astype(jnp.int32), (0, UNROLL))
    return padded, cuts.astype(jnp.int32)


def window_starts(cuts, stages, size):
    w = jnp.arange(stages + 1, dtype=jnp.int32)
    later = w[:, None] - w[None, :]
    reach = jnp.where(later >= 0, cuts[None, :] + later * size, jnp.int32(1 << 30))
    return jnp.min(reach, axis=1).astype(jnp.int32)


def paired_shards(yields, partners):
    snaps_local, columns = yields.shape
    blocks = columns // BLOCK
    snap_count, bond_count = lax.axis_size("snap"), lax.axis_size("bond")
    total_snaps = snaps_local * snap_count
    q, d = lax.axis_index("snap"), lax.axis_index("bond")
    odd = lax.rem(d, 2).astype(jnp.int32)
    slots = partners.shape[1] // snap_count
    chunk, size = CHUNK, WINDOW
    chunks = blocks // chunk
    far_blocks = REACH - 1 - blocks
    far_chunks = -(-far_blocks // chunk)
    stages = chunks + 2
    cfg = {
        "slots": slots,
        "blocks": blocks,
        "chunk": chunk,
        "window": size,
        "stages": stages,
        "cut_m": 0,
        "cut_o": stages + 1,
        "win_o": 2 * (stages + 1),
        "win_m": 3 * (stages + 1),
        "odd": 4 * (stages + 1),
        "inverse": 1.0 / (total_snaps - 1),
    }

    def other_core(value):
        return lax.ppermute(value, "snap", [(s, s ^ 1) for s in range(snap_count)])

    def other_chip(value):
        halved = value.astype(jnp.float16)
        got = lax.ppermute(halved, "snap", [(s, s ^ 2) for s in range(snap_count)])
        return got.astype(F32)

    down = [(s, s - 2) for s in range(2, bond_count)]
    to_even = [(s, s - 1) for s in range(1, bond_count, 2)]
    to_odd = [(s, s + 1) for s in range(0, bond_count, 2)]
    odd_array = odd[None]

    far, near = [None] * chunks, [None] * (chunks + 1)
    send_far0, send_far1, send_near0, mark = feed(
        cfg, (("own", 0), ("own", 1), ("own", 0)), odd_array, yields, yields
    )
    far[0] = lax.ppermute(send_far0, "bond", down)
    near[0] = lax.ppermute(send_near0, "bond", to_even)
    far[1] = lax.ppermute(send_far1, "bond", down)

    def step(t, *marks):
        last = t + 1 == chunks
        plan = ((("relay" if last else "pick"), t + 1),)
        if t + 2 < chunks:
            plan += (("own", t + 2),)
        made = feed(cfg, plan, odd_array, yields, far[t], *marks)
        near[t + 1] = lax.ppermute(made[0], "bond", to_odd if last else to_even + to_odd)
        if t + 2 < chunks:
            far[t + 2] = lax.ppermute(made[1], "bond", down)
        return made[-1]

    totals = lax.psum(column_sums(yields, mark), "snap")
    bond_means = totals / total_snaps
    near_mean = from_behind(bond_means, "bond", -1).reshape(blocks, BLOCK)
    far_mean = from_behind(bond_means, "bond", -2).reshape(blocks, BLOCK)
    xa = centered_transposed(yields, bond_means)
    xb = other_core(xa)

    rel = partners - d * blocks
    live = partners >= 0
    hop = jnp.where(rel < 2 * blocks, (rel - blocks) // chunk + odd, (rel - 2 * blocks) // chunk)
    stage = jnp.where(rel < blocks, 0, hop + 1)

    def listed(owner):
        def cut(a):
            return lax.dynamic_slice_in_dim(a, owner * slots, slots, axis=1)

        return work_list(cut(rel), cut(live), cut(stage), stages)

    mlist, mcuts = listed(q)
    olist, ocuts = listed(q ^ 2)
    mwin = window_starts(mcuts, stages, size)
    owin = window_starts(ocuts, stages, size)
    left = jnp.maximum(mcuts[-1] - mwin[-1], ocuts[-1] - owin[-1])
    trips = lax.pmax((left + size - 1) // size, ("snap", "bond"))
    info = jnp.concatenate([mcuts, ocuts, owin, mwin, odd_array, trips[None]])

    mark = step(0, mark)
    out, send, window, own_mark = own_stage(cfg, info, mlist, olist, xa, xb, mark)
    arrived = [other_chip(window)]
    mark = step(1, mark, own_mark)
    for t in range(chunks + 1):
        raw = [near[t], other_core(near[t])]
        if t < far_chunks:
            raw += [far[t], other_core(far[t])]
        merged = arrived[t - 1] if t >= 1 else None
        out, send, window, made_mark = halo_stage(
            cfg, t, info, mlist, olist, near_mean, far_mean, xa, xb, raw, merged, out, send, mark
        )
        arrived.append(other_chip(window))
        if t + 2 < chunks:
            mark = step(t + 2, mark, made_mark)
    for w in (stages - 2, stages - 1):
        out = merge(cfg, mwin[w : w + 2], mlist, arrived[w], out)

    def more(state):
        return state[0] < trips

    def turn(state):
        trip, result = state
        at = jnp.minimum(owin[-1] + trip * size, send.shape[0] - size)
        got = other_chip(lax.dynamic_slice_in_dim(send, at, size, axis=0))
        lo = jnp.minimum(mwin[-1] + trip * size, mcuts[-1])
        hi = jnp.minimum(lo + size, mcuts[-1])
        return trip + 1, merge(cfg, jnp.stack([lo, hi]), mlist, got, result)

    _, out = lax.while_loop(more, turn, (jnp.int32(0), out))
    return (bond_means, out)


def shards(yields, partners):
    blocks = yields.shape[1] // BLOCK
    snap_count, bond_count = lax.axis_size("snap"), lax.axis_size("bond")
    two_hops = blocks < REACH - 1 <= 2 * blocks
    if (
        two_hops
        and snap_count == 4
        and bond_count % 2 == 0
        and blocks % CHUNK == 0
        and partners.shape[1] % snap_count == 0
        and yields.shape[0] % BLOCK == 0
    ):
        return paired_shards(yields, partners)
    return plain_shards(yields, partners)


def solution(mesh):
    return jax.shard_map(
        shards,
        mesh=mesh,
        in_specs=(P("snap", "bond"), P("bond", None)),
        out_specs=(P("bond"), P("snap", "bond", None, None)),
        check_vma=False,
    )
```

time: 1250 us -> 466 us (0.37)
  local copies, waits for them, and re-layouts: 449 us -> 24.4 us
  waiting for transfers between devices: 533 us -> 165 us
  Pallas kernels: 0 us -> 155 us
  matrix products: 124 us -> 0 us
  loops' own time: 63.4 us -> 0.64 us
  starting transfers between devices: 8.32 us -> 59.6 us
  other arithmetic: 42.8 us -> 2.42 us
  blocking collectives: 11.2 us -> 50.9 us
    gather x32 -> x0, local copies, waits for them, and re-layouts: 339 us -> none  [block_tiles(): chosen = jnp.take(extended, index_row, axis=1)]
    ppermute x2, waiting for transfers between devices: 297 us -> 34.8 us  [from_behind(): lax.ppermute(value, axis, [(source, source + steps) for source in range(f...]
    reduce_scatter x1 -> x0, waiting for transfers between devices: 236 us -> none  [shards(): lax.psum_scatter(jnp.transpose(per_block, (1, 0, 2, 3)), 'snap', scatter_...]
    pallas_call x0 -> x23, Pallas kernels: none -> 155 us  [the longest x9 103 us: halo_stage(): pl.pallas_call(functools.partial(halo_kernel, cfg, hop, has_far, has_merg...]
    ppermute x0 -> x43, waiting for transfers between devices: none -> 131 us  [the longest x8 54.3 us: step(): lax.ppermute(made[0], 'bond', to_odd if last else to_even + to_odd)]
    dot_general x32 -> x0, matrix products: 124 us -> none  [block_tiles(): jnp.einsum('sa,scb->cab', own_block, chosen, preferred_element_type=jnp.f...]
    another operation x1, loops' own time: 63.4 us -> 0.64 us  [paired_shards(): _, out = lax.while_loop(more, turn, (jnp.int32(0), out))]
    ppermute x0 -> x43, starting transfers between devices: none -> 51.9 us  [the longest x10 13.9 us: other_chip(): got = lax.ppermute(halved, 'snap', [(s, s ^ 2) for s in range(snap_count)])]
  transfers between devices with their start and end apart: 3 -> 45, of which waited for: 2 -> 16; matrix products, arithmetic and copies ran while one was open for 0% -> 1% of each run, Pallas kernels for 0% -> 31%
where the time goes in v1:
time: 466 us; the launch traced here: 463 us
  waiting for transfers between devices  165 us (35%)
  Pallas kernels  155 us (33%)
  starting transfers between devices  59.6 us (13%)
  blocking collectives  50.9 us (11%)
  local copies, waits for them, and re-layouts  24.4 us (5%)
    pallas_call x9, Pallas kernels, halo_stage(): pl.pallas_call(functools.partial(halo_kernel, cfg, hop, has_far, has_merg...  103 us
    ppermute x8, waiting for transfers between devices, step(): lax.ppermute(made[0], 'bond', to_odd if last else to_even + to_odd)  54.3 us
    ppermute x10, waiting for transfers between devices, other_chip(): got = lax.ppermute(halved, 'snap', [(s, s ^ 2) for s in range(snap_count)])  51.6 us
    pmax x1, blocking collectives, paired_shards(): trips = lax.pmax((left + size - 1) // size, ('snap', 'bond'))  39.7 us
    ppermute x2, waiting for transfers between devices, from_behind(): lax.ppermute(value, axis, [(source, source + steps) for source in range(f...  34.8 us
    pallas_call x1, Pallas kernels, own_stage(): pl.pallas_call(functools.partial(own_kernel, cfg), in_specs=[SMEM, SMEM,...  26.7 us
    unnamed x32, local copies, waits for them, and re-layouts  20.4 us
    ppermute x1, waiting for transfers between devices, paired_shards(): far[0] = lax.ppermute(send_far0, 'bond', down)  18.8 us
  transfers between devices with their start and end apart: 45, of which 16 were waited for; matrix products, arithmetic and copies ran while one was open for 1% of the time, Pallas kernels for 31%

profile of v1, /device:TPU:24, one launch (start us, length us, event | category | flops | bytes accessed | tf_op | source)
XLA Modules:
  0.0 463.0 jit_solution(10300319835792443947)
XLA Ops:
  0.6 3.4 copy-done
  4.0 1.8 feed.9
  5.8 2.3 copy-done.1
  8.2 1.9 column_sums.1
  10.0 11.2 %psum.7 = f32[4096]{0:T(1024)S(1)} all-reduce(f32[4096]{0:T(1024)S(1)} %bitcast.43), channel_id=1, replica_groups=mesh['snap'=4,'bond'=8] {'snap'}, use_global_device_ids=true, to_apply=%region_0.0 | all-reduce | flops 4096 | bytes 32768 | tf_op jit(solution)/shard_map/psum | solution.py:586
  21.3 3.4 copy-done.2
  24.7 9.0 %center_transpose.1.xa.refs_5_ = bf16[32,128,1024]{2,1,0:T(8,128)(2,1)} custom-call(bf16[1024,4096]{1,0:T(8,128)(2,1)S(1)} %copy-done.2, f32[16,1,256]{2,1,0:T(1,128)S(1)} %bitcast.42), custom_call_target="tpu_custom_call" | custom-call | bytes 4096 | tf_op jit(solution)/shard_map/center_transpose/pallas_call | solution.py:165
  33.7 2.4 collective-permute-start.5
  36.1 3.3 collective-permute-start.4
  39.4 1.3 collective-permute-start.8
  40.7 18.8 %collective-permute-done.5.far.refs_9_ = bf16[1024,512]{1,0:T(8,128)(2,1)S(1)} collective-permute-done((bf16[1024,512]{1,0:T(8,128)(2,1)S(1)}, bf16[1024,512]{1,0:T(8,128)(2,1)S(1)}, u32[]{:S(2)}, u32[]{:S(2)}) %collective-permute-start.5) | collective-permute-done | bytes 1048608 | tf_op jit(solution)/shard_map/ppermute | solution.py:571
  59.5 3.4 copy-done.3
  62.9 1.3 feed.10
  64.2 4.5 collective-permute-start.7
  68.7 2.3 collective-permute-start.2
  71.0 33.4 %collective-permute-done.2 = f32[4096]{0:T(1024)S(1)} collective-permute-done((f32[4096]{0:T(1024)S(1)}, f32[4096]{0:T(1024)S(1)}, u32[]{:S(2)}, u32[]{:S(2)}) %collective-permute-start.2) | collective-permute-done | bytes 16416 | tf_op jit(solution)/shard_map/ppermute | solution.py:31
  104.4 5.3 %collective-permute-start.1 = (f32[4096]{0:T(1024)S(1)}, f32[4096]{0:T(1024)S(1)}, u32[]{:S(2)}, u32[]{:S(2)}) collective-permute-start(f32[4096]{0:T(1024)S(1)} %broadcast_multiply_fusion), channel_id=1, source_target_pairs={{1,0},{2,1},{3,2},{4,3},{5,4},{6,5},{7,6},{9,8},{10,9},{11,10},{12... | collective-permute-start | bytes 49160 | tf_op jit(solution)/shard_map/ppermute | solution.py:31
  109.8 1.4 collective-permute-done.1
  118.1 17.4 %collective-permute-done.11.refs_7_ = bf16[1024,512]{1,0:T(8,128)(2,1)} collective-permute-done((bf16[1024,512]{1,0:T(8,128)(2,1)}, bf16[1024,512]{1,0:T(8,128)(2,1)}, u32[]{:S(2)}, u32[]{:S(2)}) %collective-permute-start.11) | collective-permute-done | bytes 1048608 | tf_op jit(solution)/shard_map/ppermute | solution.py:581
  136.0 39.7 %pmax.7 = s32[]{:T(128)} all-reduce(s32[]{:T(128)S(6)} %select_n.72), channel_id=1, replica_groups=mesh['snap'=4,'bond'=8] {'snap','bond'}, use_global_device_ids=true, to_apply=%region_7.8 | all-reduce | flops 1 | bytes 8 | tf_op jit(solution)/shard_map/pmax | solution.py:609
  177.0 26.7 %own_tiles.1 = (f32[4,32,128,128]{3,2,1,0:T(8,128)}, f32[144,136,128]{2,1,0:T(8,128)}, f32[16,136,128]{2,1,0:T(8,128)S(1)}, f32[8,128]{1,0:T(8,128)S(1)}) custom-call(s32[46]{0:T(128)S(1)} %concatenate.3.info.refs_0_, s32[132]{0:T(256)S(1)} %pad.7.mlist.refs_1_, s32[132]{0:T(256)S(1)} %pad.8.olist.refs_2_, ...), custom_call_target="tpu_custom_call" | custom-call | bytes 65536 | tf_op jit(solution)/shard_map/own_tiles/pallas_call | solution.py:310
  203.7 3.8 copy-done.4
  207.5 2.5 feed.11
  210.1 2.3 collective-permute-start.6
  212.4 10.8 %collective-permute-start.17 = (bf16[1024,512]{1,0:T(8,128)(2,1)}, bf16[1024,512]{1,0:T(8,128)(2,1)}, u32[]{:S(2)}, u32[]{:S(2)}) collective-permute-start(bf16[1024,512]{1,0:T(8,128)(2,1)} %get-tuple-element.129), channel_id=1, source_target_pairs={{1,0},{3,2},{5,4},{7,6},{0,1},{2,3},{4,5},{6,7},{9,8},{11,10},{13,... | collective-permute-start | bytes 3145736 | tf_op jit(solution)/shard_map/ppermute | solution.py:581
  223.2 12.6 %halo_tiles.9 = (f32[4,32,128,128]{3,2,1,0:T(8,128)}, f32[144,136,128]{2,1,0:T(8,128)}, f32[16,136,128]{2,1,0:T(8,128)S(1)}, f32[8,128]{1,0:T(8,128)S(1)}) custom-call(s32[46]{0:T(128)S(1)} %concatenate.3.info.refs_0_, s32[132]{0:T(256)S(1)} %pad.7.mlist.refs_1_, s32[132]{0:T(256)S(1)} %pad.8.olist.refs_2_, ...), custom_call_target="tpu_custom_call", output_to_operand_aliasing={{0}: (11, {}), {1}: (12, {})} | custom-call | bytes 65536 | tf_op jit(solution)/shard_map/halo_tiles/pallas_call | solution.py:458
  237.2 3.7 collective-permute-start.14
  240.9 1.3 collective-permute-start.16
  242.3 9.4 %collective-permute-done.14 = f16[16,136,128]{2,1,0:T(8,128)(2,1)S(1)} collective-permute-done((f16[16,136,128]{2,1,0:T(8,128)(2,1)S(1)}, f16[16,136,128]{2,1,0:T(8,128)(2,1)S(1)}, u32[]{:S(2)}, u32[]{:S(2)}) %collective-permute-start.14) | collective-permute-done | bytes 557088 | tf_op jit(solution)/shard_map/ppermute | solution.py:559
  251.8 2.5 collective-permute-start.20
  254.3 13.7 %halo_tiles.10 = (f32[4,32,128,128]{3,2,1,0:T(8,128)}, f32[144,136,128]{2,1,0:T(8,128)}, f32[16,136,128]{2,1,0:T(8,128)S(1)}, f32[8,128]{1,0:T(8,128)S(1)}) custom-call(s32[46]{0:T(128)S(1)} %concatenate.3.info.refs_0_, s32[132]{0:T(256)S(1)} %pad.7.mlist.refs_1_, s32[132]{0:T(256)S(1)} %pad.8.olist.refs_2_, ...), custom_call_target="tpu_custom_call", output_to_operand_aliasing={{0}: (12, {}), {1}: (13, {})} | custom-call | bytes 65536 | tf_op jit(solution)/shard_map/halo_tiles/pallas_call | solution.py:458
  268.8 2.1 feed.13
  271.2 6.6 %collective-permute-done.24 = f16[16,136,128]{2,1,0:T(8,128)(2,1)S(1)} collective-permute-done((f16[16,136,128]{2,1,0:T(8,128)(2,1)S(1)}, f16[16,136,128]{2,1,0:T(8,128)(2,1)S(1)}, u32[]{:S(2)}, u32[]{:S(2)}) %collective-permute-start.24) | collective-permute-done | bytes 557088 | tf_op jit(solution)/shard_map/ppermute | solution.py:559
  277.7 1.3 collective-permute-start.15
  279.3 13.4 %halo_tiles.11 = (f32[4,32,128,128]{3,2,1,0:T(8,128)}, f32[144,136,128]{2,1,0:T(8,128)}, f32[16,136,128]{2,1,0:T(8,128)S(1)}, f32[8,128]{1,0:T(8,128)S(1)}) custom-call(s32[46]{0:T(128)S(1)} %concatenate.3.info.refs_0_, s32[132]{0:T(256)S(1)} %pad.7.mlist.refs_1_, s32[132]{0:T(256)S(1)} %pad.8.olist.refs_2_, ...), custom_call_target="tpu_custom_call", output_to_operand_aliasing={{0}: (12, {}), {1}: (13, {})} | custom-call | bytes 65536 | tf_op jit(solution)/shard_map/halo_tiles/pallas_call | solution.py:458
  292.7 1.3 feed.14
  294.2 2.9 collective-permute-done.27.refs_7_
  297.2 1.0 copy-done.9
  298.2 2.1 collective-permute-start.30
  300.2 1.2 copy-done.10
  301.5 12.0 %halo_tiles.12 = (f32[4,32,128,128]{3,2,1,0:T(8,128)}, f32[144,136,128]{2,1,0:T(8,128)}, f32[16,136,128]{2,1,0:T(8,128)S(1)}, f32[8,128]{1,0:T(8,128)S(1)}) custom-call(s32[46]{0:T(128)S(1)} %concatenate.3.info.refs_0_, s32[132]{0:T(256)S(1)} %pad.7.mlist.refs_1_, s32[132]{0:T(256)S(1)} %pad.8.olist.refs_2_, ...), custom_call_target="tpu_custom_call", output_to_operand_aliasing={{0}: (12, {}), {1}: (13, {})} | custom-call | bytes 65536 | tf_op jit(solution)/shard_map/halo_tiles/pallas_call | solution.py:458
  313.7 1.4 collective-permute-start.26
  315.1 2.2 collective-permute-start.33
  317.3 1.5 collective-permute-done.31.refs_7_
  318.8 1.7 feed.15
  320.5 7.5 %collective-permute-done.34 = f16[16,136,128]{2,1,0:T(8,128)(2,1)S(1)} collective-permute-done((f16[16,136,128]{2,1,0:T(8,128)(2,1)S(1)}, f16[16,136,128]{2,1,0:T(8,128)(2,1)S(1)}, u32[]{:S(2)}, u32[]{:S(2)}) %collective-permute-start.34) | collective-permute-done | bytes 557088 | tf_op jit(solution)/shard_map/ppermute | solution.py:559
  328.0 1.3 collective-permute-start.25
  329.6 12.5 %halo_tiles.13 = (f32[4,32,128,128]{3,2,1,0:T(8,128)}, f32[144,136,128]{2,1,0:T(8,128)}, f32[16,136,128]{2,1,0:T(8,128)S(1)}, f32[8,128]{1,0:T(8,128)S(1)}) custom-call(s32[46]{0:T(128)S(1)} %concatenate.3.info.refs_0_, s32[132]{0:T(256)S(1)} %pad.7.mlist.refs_1_, s32[132]{0:T(256)S(1)} %pad.8.olist.refs_2_, ...), custom_call_target="tpu_custom_call", output_to_operand_aliasing={{0}: (12, {}), {1}: (13, {})} | custom-call | bytes 65536 | tf_op jit(solution)/shard_map/halo_tiles/pallas_call | solution.py:458
  342.7 11.2 %halo_tiles.14 = (f32[4,32,128,128]{3,2,1,0:T(8,128)}, f32[144,136,128]{2,1,0:T(8,128)}, f32[16,136,128]{2,1,0:T(8,128)S(1)}, f32[8,128]{1,0:T(8,128)S(1)}) custom-call(s32[46]{0:T(128)S(1)} %concatenate.3.info.refs_0_, s32[132]{0:T(256)S(1)} %pad.7.mlist.refs_1_, s32[132]{0:T(256)S(1)} %pad.8.olist.refs_2_, ...), custom_call_target="tpu_custom_call", output_to_operand_aliasing={{0}: (12, {}), {1}: (13, {})} | custom-call | bytes 65536 | tf_op jit(solution)/shard_map/halo_tiles/pallas_call | solution.py:458
  353.9 5.9 %collective-permute-done.25.far = bf16[1024,512]{1,0:T(8,128)(2,1)S(1)} collective-permute-done((bf16[1024,512]{1,0:T(8,128)(2,1)}, bf16[1024,512]{1,0:T(8,128)(2,1)S(1)}, u32[]{:S(2)}, u32[]{:S(2)}) %collective-permute-start.25) | collective-permute-done | bytes 1048608 | tf_op jit(solution)/shard_map/ppermute | solution.py:583
  360.0 1.4 collective-permute-start.35
  361.4 1.7 collective-permute-start.38
  363.2 2.1 collective-permute-start.39
  365.3 12.9 %collective-permute-done.41.refs_7_ = bf16[1024,512]{1,0:T(8,128)(2,1)} collective-permute-done((bf16[1024,512]{1,0:T(8,128)(2,1)S(1)}, bf16[1024,512]{1,0:T(8,128)(2,1)}, u32[]{:S(2)}, u32[]{:S(2)}) %collective-permute-start.41) | collective-permute-done | bytes 1048608 | tf_op jit(solution)/shard_map/ppermute | solution.py:581
  378.3 19.5 %collective-permute-done.35.refs_7_ = bf16[1024,512]{1,0:T(8,128)(2,1)S(1)} collective-permute-done((bf16[1024,512]{1,0:T(8,128)(2,1)S(1)}, bf16[1024,512]{1,0:T(8,128)(2,1)S(1)}, u32[]{:S(2)}, u32[]{:S(2)}) %collective-permute-start.35) | collective-permute-done | bytes 1048608 | tf_op jit(solution)/shard_map/ppermute | solution.py:581
  398.5 1.2 copy-done.8
  399.7 11.6 %halo_tiles.15 = (f32[4,32,128,128]{3,2,1,0:T(8,128)}, f32[144,136,128]{2,1,0:T(8,128)}, f32[16,136,128]{2,1,0:T(8,128)S(1)}, f32[8,128]{1,0:T(8,128)}) custom-call(s32[46]{0:T(128)S(1)} %concatenate.3.info.refs_0_, s32[132]{0:T(256)S(1)} %pad.7.mlist.refs_1_, s32[132]{0:T(256)S(1)} %pad.8.olist.refs_2_, ...), custom_call_target="tpu_custom_call", output_to_operand_aliasing={{0}: (10, {}), {1}: (11, {})} | custom-call | bytes 65536 | tf_op jit(solution)/shard_map/halo_tiles/pallas_call | solution.py:458
  413.2 11.8 %collective-permute-done.40 = f16[16,136,128]{2,1,0:T(8,128)(2,1)S(1)} collective-permute-done((f16[16,136,128]{2,1,0:T(8,128)(2,1)S(1)}, f16[16,136,128]{2,1,0:T(8,128)(2,1)S(1)}, u32[]{:S(2)}, u32[]{:S(2)}) %collective-permute-start.40) | collective-permute-done | bytes 557088 | tf_op jit(solution)/shard_map/ppermute | solution.py:559
  425.1 11.9 %halo_tiles.16 = (f32[4,32,128,128]{3,2,1,0:T(8,128)}, f32[144,136,128]{2,1,0:T(8,128)}, f32[16,136,128]{2,1,0:T(8,128)S(1)}, f32[8,128]{1,0:T(8,128)}) custom-call(s32[46]{0:T(128)S(1)} %concatenate.3.info.refs_0_, s32[132]{0:T(256)S(1)} %pad.7.mlist.refs_1_, s32[132]{0:T(256)S(1)} %pad.8.olist.refs_2_, ...), custom_call_target="tpu_custom_call", output_to_operand_aliasing={{0}: (10, {}), {1}: (11, {})} | custom-call | bytes 65536 | tf_op jit(solution)/shard_map/halo_tiles/pallas_call | solution.py:458
  437.7 3.6 halo_tiles.17
  441.4 1.9 collective-permute-start.44
  443.4 9.3 %collective-permute-done.45 = f16[16,136,128]{2,1,0:T(8,128)(2,1)S(1)} collective-permute-done((f16[16,136,128]{2,1,0:T(8,128)(2,1)S(1)}, f16[16,136,128]{2,1,0:T(8,128)(2,1)S(1)}, u32[]{:S(2)}, u32[]{:S(2)}) %collective-permute-start.45) | collective-permute-done | bytes 557088 | tf_op jit(solution)/shard_map/ppermute | solution.py:559
  452.8 2.3 merge_tiles.3._
  455.1 6.1 %collective-permute-done.44 = f16[16,136,128]{2,1,0:T(8,128)(2,1)S(1)} collective-permute-done((f16[16,136,128]{2,1,0:T(8,128)(2,1)S(1)}, f16[16,136,128]{2,1,0:T(8,128)(2,1)S(1)}, u32[]{:S(2)}, u32[]{:S(2)}) %collective-permute-start.44) | collective-permute-done | bytes 557088 | tf_op jit(solution)/shard_map/ppermute | solution.py:559
  (136 shorter events, 15.3 us)
Async XLA Ops:
  0.6 3.4 copy-start
  4.0 4.1 copy-start.1
  21.3 83.1 %copy-start.11 = (f32[4096]{0:T(1024)}, f32[4096]{0:T(1024)S(1)}, u32[]{:S(2)}) copy-start(f32[4096]{0:T(1024)S(1)} %broadcast_multiply_fusion) | copy-start | bytes 49156
  21.3 3.4 copy-start.2
  24.7 44.0 %copy-start.13 = (s32[32,16]{0,1:T(8,128)S(1)}, s32[32,16]{0,1:T(8,128)}, u32[]{:S(2)}) copy-start(s32[32,16]{0,1:T(8,128)} %param.5) | copy-start | bytes 6148
  33.7 101.7 %collective-permute-start.3 = (bf16[32,128,1024]{2,1,0:T(8,128)(2,1)}, bf16[32,128,1024]{2,1,0:T(8,128)(2,1)}, u32[]{:S(2)}, u32[]{:S(2)}) collective-permute-start(bf16[32,128,1024]{2,1,0:T(8,128)(2,1)} %center_transpose.1.xa.refs_5_), channel_id=1, source_target_pairs={{0,8},{8,0},{16,24},{24,16},{1,9},{9,1},{17,25},{25,17},{2,10},{10... | collective-permute-start | bytes 25165832 | tf_op jit(solution)/shard_map/ppermute | solution.py:555
  33.7 25.8 %collective-permute-start.5 = (bf16[1024,512]{1,0:T(8,128)(2,1)S(1)}, bf16[1024,512]{1,0:T(8,128)(2,1)S(1)}, u32[]{:S(2)}, u32[]{:S(2)}) collective-permute-start(bf16[1024,512]{1,0:T(8,128)(2,1)S(1)} %get-tuple-element.110), channel_id=1, source_target_pairs={{2,0},{3,1},{4,2},{5,3},{6,4},{7,5},{10,8},{11,9},{12,10},{13,11},... | collective-permute-start | bytes 3145736 | tf_op jit(solution)/shard_map/ppermute | solution.py:571
  36.1 75.5 %collective-permute-start.4 = (bf16[1024,512]{1,0:T(8,128)(2,1)}, bf16[1024,512]{1,0:T(8,128)(2,1)}, u32[]{:S(2)}, u32[]{:S(2)}) collective-permute-start(bf16[1024,512]{1,0:T(8,128)(2,1)} %get-tuple-element.109), channel_id=1, source_target_pairs={{2,0},{3,1},{4,2},{5,3},{6,4},{7,5},{10,8},{11,9},{12,10},{13,11},... | collective-permute-start | bytes 3145736 | tf_op jit(solution)/shard_map/ppermute | solution.py:573
  39.4 73.7 %collective-permute-start.8 = (bf16[1024,512]{1,0:T(8,128)(2,1)}, bf16[1024,512]{1,0:T(8,128)(2,1)}, u32[]{:S(2)}, u32[]{:S(2)}) collective-permute-start(bf16[1024,512]{1,0:T(8,128)(2,1)} %get-tuple-element.116), channel_id=1, source_target_pairs={{1,0},{3,2},{5,4},{7,6},{9,8},{11,10},{13,12},{15,14},{17,16},{19,... | collective-permute-start | bytes 3145736 | tf_op jit(solution)/shard_map/ppermute | solution.py:572
  59.5 3.4 copy-start.3
  64.2 4.5 copy-start.12
  64.2 49.4 %collective-permute-start.7 = (bf16[1024,512]{1,0:T(8,128)(2,1)}, bf16[1024,512]{1,0:T(8,128)(2,1)S(1)}, u32[]{:S(2)}, u32[]{:S(2)}) collective-permute-start(bf16[1024,512]{1,0:T(8,128)(2,1)} %get-tuple-element.114), channel_id=1, source_target_pairs={{2,0},{3,1},{4,2},{5,3},{6,4},{7,5},{10,8},{11,9},{12,10},{13,11},... | collective-permute-start | bytes 3145736 | tf_op jit(solution)/shard_map/ppermute | solution.py:583
  68.7 35.7 %collective-permute-start.2 = (f32[4096]{0:T(1024)S(1)}, f32[4096]{0:T(1024)S(1)}, u32[]{:S(2)}, u32[]{:S(2)}) collective-permute-start(f32[4096]{0:T(1024)S(1)} %broadcast_multiply_fusion), channel_id=1, source_target_pairs={{2,0},{3,1},{4,2},{5,3},{6,4},{7,5},{10,8},{11,9},{12,10},{13,11},... | collective-permute-start | bytes 49160 | tf_op jit(solution)/shard_map/ppermute | solution.py:31
  104.4 6.8 %collective-permute-start.1 = (f32[4096]{0:T(1024)S(1)}, f32[4096]{0:T(1024)S(1)}, u32[]{:S(2)}, u32[]{:S(2)}) collective-permute-start(f32[4096]{0:T(1024)S(1)} %broadcast_multiply_fusion), channel_id=1, source_target_pairs={{1,0},{2,1},{3,2},{4,3},{5,4},{6,5},{7,6},{9,8},{10,9},{11,10},{12... | collective-permute-start | bytes 49160 | tf_op jit(solution)/shard_map/ppermute | solution.py:31
  111.2 24.3 %collective-permute-start.11 = (bf16[1024,512]{1,0:T(8,128)(2,1)}, bf16[1024,512]{1,0:T(8,128)(2,1)}, u32[]{:S(2)}, u32[]{:S(2)}) collective-permute-start(bf16[1024,512]{1,0:T(8,128)(2,1)} %copy-done.12), channel_id=1, source_target_pairs={{1,0},{3,2},{5,4},{7,6},{0,1},{2,3},{4,5},{6,7},{9,8},{11,10},{13,... | collective-permute-start | bytes 3145736 | tf_op jit(solution)/shard_map/ppermute | solution.py:581
  111.6 98.5 %collective-permute-start.10 = (bf16[1024,512]{1,0:T(8,128)(2,1)S(1)}, bf16[1024,512]{1,0:T(8,128)(2,1)}, u32[]{:S(2)}, u32[]{:S(2)}) collective-permute-start(bf16[1024,512]{1,0:T(8,128)(2,1)S(1)} %collective-permute-done.5.far.refs_9_), channel_id=1, source_target_pairs={{0,8},{8,0},{16,24},{24,16},{1,9},{9,1},{17,25},{25,17},{2,10},{10... | collective-permute-start | bytes 3145736 | tf_op jit(solution)/shard_map/ppermute | solution.py:555
  113.1 99.3 %collective-permute-start.9 = (bf16[1024,512]{1,0:T(8,128)(2,1)}, bf16[1024,512]{1,0:T(8,128)(2,1)}, u32[]{:S(2)}, u32[]{:S(2)}) collective-permute-start(bf16[1024,512]{1,0:T(8,128)(2,1)} %collective-permute-done.8.refs_7_), channel_id=1, source_target_pairs={{0,8},{8,0},{16,24},{24,16},{1,9},{9,1},{17,25},{25,17},{2,10},{10... | collective-permute-start | bytes 3145736 | tf_op jit(solution)/shard_map/ppermute | solution.py:555
  113.6 122.8 %collective-permute-start.13 = (bf16[1024,512]{1,0:T(8,128)(2,1)}, bf16[1024,512]{1,0:T(8,128)(2,1)}, u32[]{:S(2)}, u32[]{:S(2)}) collective-permute-start(bf16[1024,512]{1,0:T(8,128)(2,1)} %collective-permute-done.4.far.refs_9_), channel_id=1, source_target_pairs={{0,8},{8,0},{16,24},{24,16},{1,9},{9,1},{17,25},{25,17},{2,10},{10... | collective-permute-start | bytes 3145736 | tf_op jit(solution)/shard_map/ppermute | solution.py:555
  135.4 101.7 %collective-permute-start.12 = (bf16[1024,512]{1,0:T(8,128)(2,1)}, bf16[1024,512]{1,0:T(8,128)(2,1)}, u32[]{:S(2)}, u32[]{:S(2)}) collective-permute-start(bf16[1024,512]{1,0:T(8,128)(2,1)} %collective-permute-done.11.refs_7_), channel_id=1, source_target_pairs={{0,8},{8,0},{16,24},{24,16},{1,9},{9,1},{17,25},{25,17},{2,10},{10... | collective-permute-start | bytes 3145736 | tf_op jit(solution)/shard_map/ppermute | solution.py:555
  135.4 105.5 %collective-permute-start.19 = (bf16[1024,512]{1,0:T(8,128)(2,1)S(1)}, bf16[1024,512]{1,0:T(8,128)(2,1)}, u32[]{:S(2)}, u32[]{:S(2)}) collective-permute-start(bf16[1024,512]{1,0:T(8,128)(2,1)S(1)} %collective-permute-done.7.far.refs_9_), channel_id=1, source_target_pairs={{0,8},{8,0},{16,24},{24,16},{1,9},{9,1},{17,25},{25,17},{2,10},{10... | collective-permute-start | bytes 3145736 | tf_op jit(solution)/shard_map/ppermute | solution.py:555
  203.7 6.4 %copy-start.5 = (f32[16,136,128]{2,1,0:T(8,128)}, f32[16,136,128]{2,1,0:T(8,128)S(1)}, u32[]{:S(2)}) copy-start(f32[16,136,128]{2,1,0:T(8,128)S(1)} %get-tuple-element.122) | copy-start | bytes 3342340
  203.7 3.8 copy-start.4
  207.5 28.3 %slice-start = ((s8[8388608]{0:T(1024)(128)(4,1)}), s8[4194304]{0:T(1024)(128)(4,1)S(1)}, s32[]{:S(2)}) async-start(s8[8388608]{0:T(1024)(128)(4,1)} %bitcast.22), calls=%async_computation | async-start | bytes 8388608
  210.1 58.1 %collective-permute-start.6 = (bf16[1024,512]{1,0:T(8,128)(2,1)}, bf16[1024,512]{1,0:T(8,128)(2,1)}, u32[]{:S(2)}, u32[]{:S(2)}) collective-permute-start(bf16[1024,512]{1,0:T(8,128)(2,1)} %get-tuple-element.113), channel_id=1, source_target_pairs={{2,0},{3,1},{4,2},{5,3},{6,4},{7,5},{10,8},{11,9},{12,10},{13,11},... | collective-permute-start | bytes 3145736 | tf_op jit(solution)/shard_map/ppermute | solution.py:583
  212.4 55.9 %collective-permute-start.17 = (bf16[1024,512]{1,0:T(8,128)(2,1)}, bf16[1024,512]{1,0:T(8,128)(2,1)}, u32[]{:S(2)}, u32[]{:S(2)}) collective-permute-start(bf16[1024,512]{1,0:T(8,128)(2,1)} %get-tuple-element.129), channel_id=1, source_target_pairs={{1,0},{3,2},{5,4},{7,6},{0,1},{2,3},{4,5},{6,7},{9,8},{11,10},{13,... | collective-permute-start | bytes 3145736 | tf_op jit(solution)/shard_map/ppermute | solution.py:581
  223.2 12.7 %slice-start.1 = ((s8[8388608]{0:T(1024)(128)(4,1)}), s8[4194304]{0:T(1024)(128)(4,1)S(1)}, s32[]{:S(2)}) async-start(s8[8388608]{0:T(1024)(128)(4,1)} %bitcast.22), calls=%async_computation.1 | async-start | bytes 8388608
  235.8 1.2 copy-start.6
  236.4 31.9 %collective-permute-start.21 = (bf16[1024,512]{1,0:T(8,128)(2,1)S(1)}, bf16[1024,512]{1,0:T(8,128)(2,1)S(1)}, u32[]{:S(2)}, u32[]{:S(2)}) collective-permute-start(bf16[1024,512]{1,0:T(8,128)(2,1)S(1)} %get-tuple-element.135), channel_id=1, source_target_pairs={{1,0},{3,2},{5,4},{7,6},{0,1},{2,3},{4,5},{6,7},{9,8},{11,10},{13,... | collective-permute-start | bytes 3145736 | tf_op jit(solution)/shard_map/ppermute | solution.py:581
  237.2 14.6 %collective-permute-start.14 = (f16[16,136,128]{2,1,0:T(8,128)(2,1)S(1)}, f16[16,136,128]{2,1,0:T(8,128)(2,1)S(1)}, u32[]{:S(2)}, u32[]{:S(2)}) collective-permute-start(f16[16,136,128]{2,1,0:T(8,128)(2,1)S(1)} %convert_element_type.82), channel_id=1, source_target_pairs={{0,16},{8,24},{16,0},{24,8},{1,17},{9,25},{17,1},{25,9},{2,18},{10... | collective-permute-start | bytes 1671176 | tf_op jit(solution)/shard_map/ppermute | solution.py:559
  240.9 30.1 %collective-permute-start.16 = (bf16[1024,512]{1,0:T(8,128)(2,1)S(1)}, bf16[1024,512]{1,0:T(8,128)(2,1)S(1)}, u32[]{:S(2)}, u32[]{:S(2)}) collective-permute-start(bf16[1024,512]{1,0:T(8,128)(2,1)S(1)} %get-tuple-element.127), channel_id=1, source_target_pairs={{2,0},{3,1},{4,2},{5,3},{6,4},{7,5},{10,8},{11,9},{12,10},{13,11},... | collective-permute-start | bytes 3145736 | tf_op jit(solution)/shard_map/ppermute | solution.py:583
  251.8 19.1 %collective-permute-start.20 = (f16[16,136,128]{2,1,0:T(8,128)(2,1)S(1)}, f16[16,136,128]{2,1,0:T(8,128)(2,1)S(1)}, u32[]{:S(2)}, u32[]{:S(2)}) collective-permute-start(f16[16,136,128]{2,1,0:T(8,128)(2,1)S(1)} %convert_element_type.84), channel_id=1, source_target_pairs={{0,16},{8,24},{16,0},{24,8},{1,17},{9,25},{17,1},{25,9},{2,18},{10... | collective-permute-start | bytes 1671176 | tf_op jit(solution)/shard_map/ppermute | solution.py:559
  268.2 9.6 %collective-permute-start.24 = (f16[16,136,128]{2,1,0:T(8,128)(2,1)S(1)}, f16[16,136,128]{2,1,0:T(8,128)(2,1)S(1)}, u32[]{:S(2)}, u32[]{:S(2)}) collective-permute-start(f16[16,136,128]{2,1,0:T(8,128)(2,1)S(1)} %convert_element_type.86), channel_id=1, source_target_pairs={{0,16},{8,24},{16,0},{24,8},{1,17},{9,25},{17,1},{25,9},{2,18},{10... | collective-permute-start | bytes 1671176 | tf_op jit(solution)/shard_map/ppermute | solution.py:559
  268.2 10.9 %collective-permute-start.18 = (bf16[1024,512]{1,0:T(8,128)(2,1)}, bf16[1024,512]{1,0:T(8,128)(2,1)S(1)}, u32[]{:S(2)}, u32[]{:S(2)}) collective-permute-start(bf16[1024,512]{1,0:T(8,128)(2,1)} %collective-permute-done.17.refs_7_), channel_id=1, source_target_pairs={{0,8},{8,0},{16,24},{24,16},{1,9},{9,1},{17,25},{25,17},{2,10},{10... | collective-permute-start | bytes 3145736 | tf_op jit(solution)/shard_map/ppermute | solution.py:555
  268.3 25.7 %collective-permute-start.22 = (bf16[1024,512]{1,0:T(8,128)(2,1)S(1)}, bf16[1024,512]{1,0:T(8,128)(2,1)S(1)}, u32[]{:S(2)}, u32[]{:S(2)}) collective-permute-start(bf16[1024,512]{1,0:T(8,128)(2,1)S(1)} %collective-permute-done.21.refs_7_), channel_id=1, source_target_pairs={{0,8},{8,0},{16,24},{24,16},{1,9},{9,1},{17,25},{25,17},{2,10},{10... | collective-permute-start | bytes 3145736 | tf_op jit(solution)/shard_map/ppermute | solution.py:555
  270.9 26.2 %collective-permute-start.27 = (bf16[1024,512]{1,0:T(8,128)(2,1)}, bf16[1024,512]{1,0:T(8,128)(2,1)S(1)}, u32[]{:S(2)}, u32[]{:S(2)}) collective-permute-start(bf16[1024,512]{1,0:T(8,128)(2,1)} %get-tuple-element.143), channel_id=1, source_target_pairs={{1,0},{3,2},{5,4},{7,6},{0,1},{2,3},{4,5},{6,7},{9,8},{11,10},{13,... | collective-permute-start | bytes 3145736 | tf_op jit(solution)/shard_map/ppermute | solution.py:581
  271.0 26.2 %collective-permute-start.23 = (bf16[1024,512]{1,0:T(8,128)(2,1)}, bf16[1024,512]{1,0:T(8,128)(2,1)S(1)}, u32[]{:S(2)}, u32[]{:S(2)}) collective-permute-start(bf16[1024,512]{1,0:T(8,128)(2,1)} %collective-permute-done.6.far.refs_9_), channel_id=1, source_target_pairs={{0,8},{8,0},{16,24},{24,16},{1,9},{9,1},{17,25},{25,17},{2,10},{10... | collective-permute-start | bytes 3145736 | tf_op jit(solution)/shard_map/ppermute | solution.py:555
  277.7 35.8 %collective-permute-start.15 = (bf16[1024,512]{1,0:T(8,128)(2,1)S(1)}, bf16[1024,512]{1,0:T(8,128)(2,1)S(1)}, u32[]{:S(2)}, u32[]{:S(2)}) collective-permute-start(bf16[1024,512]{1,0:T(8,128)(2,1)S(1)} %get-tuple-element.126), channel_id=1, source_target_pairs={{2,0},{3,1},{4,2},{5,3},{6,4},{7,5},{10,8},{11,9},{12,10},{13,11},... | collective-permute-start | bytes 3145736 | tf_op jit(solution)/shard_map/ppermute | solution.py:583
  279.2 34.5 %collective-permute-start.29 = (bf16[1024,512]{1,0:T(8,128)(2,1)S(1)}, bf16[1024,512]{1,0:T(8,128)(2,1)S(1)}, u32[]{:S(2)}, u32[]{:S(2)}) collective-permute-start(bf16[1024,512]{1,0:T(8,128)(2,1)S(1)} %collective-permute-done.16.far.refs_9_), channel_id=1, source_target_pairs={{0,8},{8,0},{16,24},{24,16},{1,9},{9,1},{17,25},{25,17},{2,10},{10... | collective-permute-start | bytes 3145736 | tf_op jit(solution)/shard_map/ppermute | solution.py:555
  294.0 24.8 %collective-permute-start.31 = (bf16[1024,512]{1,0:T(8,128)(2,1)S(1)}, bf16[1024,512]{1,0:T(8,128)(2,1)S(1)}, u32[]{:S(2)}, u32[]{:S(2)}) collective-permute-start(bf16[1024,512]{1,0:T(8,128)(2,1)S(1)} %get-tuple-element.149), channel_id=1, source_target_pairs={{1,0},{3,2},{5,4},{7,6},{0,1},{2,3},{4,5},{6,7},{9,8},{11,10},{13,... | collective-permute-start | bytes 3145736 | tf_op jit(solution)/shard_map/ppermute | solution.py:581
  297.1 32.2 %collective-permute-start.28 = (bf16[1024,512]{1,0:T(8,128)(2,1)S(1)}, bf16[1024,512]{1,0:T(8,128)(2,1)S(1)}, u32[]{:S(2)}, u32[]{:S(2)}) collective-permute-start(bf16[1024,512]{1,0:T(8,128)(2,1)S(1)} %collective-permute-done.27.refs_7_), channel_id=1, source_target_pairs={{0,8},{8,0},{16,24},{24,16},{1,9},{9,1},{17,25},{25,17},{2,10},{10... | collective-permute-start | bytes 3145736 | tf_op jit(solution)/shard_map/ppermute | solution.py:555
  297.2 1.0 copy-start.9
  298.2 16.9 %collective-permute-start.30 = (f16[16,136,128]{2,1,0:T(8,128)(2,1)S(1)}, f16[16,136,128]{2,1,0:T(8,128)(2,1)S(1)}, u32[]{:S(2)}, u32[]{:S(2)}) collective-permute-start(f16[16,136,128]{2,1,0:T(8,128)(2,1)S(1)} %convert_element_type.88), channel_id=1, source_target_pairs={{0,16},{8,24},{16,0},{24,8},{1,17},{9,25},{17,1},{25,9},{2,18},{10... | collective-permute-start | bytes 1671176 | tf_op jit(solution)/shard_map/ppermute | solution.py:559
  300.2 1.2 copy-start.10
  313.6 14.4 %collective-permute-start.34 = (f16[16,136,128]{2,1,0:T(8,128)(2,1)S(1)}, f16[16,136,128]{2,1,0:T(8,128)(2,1)S(1)}, u32[]{:S(2)}, u32[]{:S(2)}) collective-permute-start(f16[16,136,128]{2,1,0:T(8,128)(2,1)S(1)} %convert_element_type.90), channel_id=1, source_target_pairs={{0,16},{8,24},{16,0},{24,8},{1,17},{9,25},{17,1},{25,9},{2,18},{10... | collective-permute-start | bytes 1671176 | tf_op jit(solution)/shard_map/ppermute | solution.py:559
  313.7 28.4 %collective-permute-start.26 = (bf16[1024,512]{1,0:T(8,128)(2,1)}, bf16[1024,512]{1,0:T(8,128)(2,1)S(1)}, u32[]{:S(2)}, u32[]{:S(2)}) collective-permute-start(bf16[1024,512]{1,0:T(8,128)(2,1)} %get-tuple-element.141), channel_id=1, source_target_pairs={{2,0},{3,1},{4,2},{5,3},{6,4},{7,5},{10,8},{11,9},{12,10},{13,11},... | collective-permute-start | bytes 3145736 | tf_op jit(solution)/shard_map/ppermute | solution.py:583
  315.1 27.6 %collective-permute-start.33 = (bf16[1024,512]{1,0:T(8,128)(2,1)S(1)}, bf16[1024,512]{1,0:T(8,128)(2,1)S(1)}, u32[]{:S(2)}, u32[]{:S(2)}) collective-permute-start(bf16[1024,512]{1,0:T(8,128)(2,1)S(1)} %collective-permute-done.15.far.refs_9_), channel_id=1, source_target_pairs={{0,8},{8,0},{16,24},{24,16},{1,9},{9,1},{17,25},{25,17},{2,10},{10... | collective-permute-start | bytes 3145736 | tf_op jit(solution)/shard_map/ppermute | solution.py:555
  318.8 23.9 %collective-permute-start.32 = (bf16[1024,512]{1,0:T(8,128)(2,1)S(1)}, bf16[1024,512]{1,0:T(8,128)(2,1)S(1)}, u32[]{:S(2)}, u32[]{:S(2)}) collective-permute-start(bf16[1024,512]{1,0:T(8,128)(2,1)S(1)} %collective-permute-done.31.refs_7_), channel_id=1, source_target_pairs={{0,8},{8,0},{16,24},{24,16},{1,9},{9,1},{17,25},{25,17},{2,10},{10... | collective-permute-start | bytes 3145736 | tf_op jit(solution)/shard_map/ppermute | solution.py:555
  328.0 31.8 %collective-permute-start.25 = (bf16[1024,512]{1,0:T(8,128)(2,1)}, bf16[1024,512]{1,0:T(8,128)(2,1)S(1)}, u32[]{:S(2)}, u32[]{:S(2)}) collective-permute-start(bf16[1024,512]{1,0:T(8,128)(2,1)} %get-tuple-element.140), channel_id=1, source_target_pairs={{2,0},{3,1},{4,2},{5,3},{6,4},{7,5},{10,8},{11,9},{12,10},{13,11},... | collective-permute-start | bytes 3145736 | tf_op jit(solution)/shard_map/ppermute | solution.py:583
  329.3 32.1 %collective-permute-start.37 = (bf16[1024,512]{1,0:T(8,128)(2,1)}, bf16[1024,512]{1,0:T(8,128)(2,1)S(1)}, u32[]{:S(2)}, u32[]{:S(2)}) collective-permute-start(bf16[1024,512]{1,0:T(8,128)(2,1)} %get-tuple-element.155), channel_id=1, source_target_pairs={{1,0},{3,2},{5,4},{7,6},{0,1},{2,3},{4,5},{6,7},{9,8},{11,10},{13,... | collective-permute-start | bytes 3145736 | tf_op jit(solution)/shard_map/ppermute | solution.py:581
  342.6 35.6 %collective-permute-start.41 = (bf16[1024,512]{1,0:T(8,128)(2,1)S(1)}, bf16[1024,512]{1,0:T(8,128)(2,1)}, u32[]{:S(2)}, u32[]{:S(2)}) collective-permute-start(bf16[1024,512]{1,0:T(8,128)(2,1)S(1)} %get-tuple-element.161), channel_id=1, source_target_pairs={{1,0},{3,2},{5,4},{7,6},{0,1},{2,3},{4,5},{6,7},{9,8},{11,10},{13,... | collective-permute-start | bytes 3145736 | tf_op jit(solution)/shard_map/ppermute | solution.py:581
  360.0 37.8 %collective-permute-start.35 = (bf16[1024,512]{1,0:T(8,128)(2,1)S(1)}, bf16[1024,512]{1,0:T(8,128)(2,1)S(1)}, u32[]{:S(2)}, u32[]{:S(2)}) collective-permute-start(bf16[1024,512]{1,0:T(8,128)(2,1)S(1)} %get-tuple-element.154), channel_id=1, source_target_pairs={{0,1},{2,3},{4,5},{6,7},{8,9},{10,11},{12,13},{14,15},{16,17},{18,... | collective-permute-start | bytes 3145736 | tf_op jit(solution)/shard_map/ppermute | solution.py:581
  361.4 37.1 %copy-start.7 = (bf16[1024,512]{1,0:T(8,128)(2,1)}, bf16[1024,512]{1,0:T(8,128)(2,1)S(1)}, u32[]{:S(2)}) copy-start(bf16[1024,512]{1,0:T(8,128)(2,1)S(1)} %collective-permute-done.37.refs_7_) | copy-start | bytes 3145732
  361.4 37.1 %collective-permute-start.38 = (bf16[1024,512]{1,0:T(8,128)(2,1)S(1)}, bf16[1024,512]{1,0:T(8,128)(2,1)S(1)}, u32[]{:S(2)}, u32[]{:S(2)}) collective-permute-start(bf16[1024,512]{1,0:T(8,128)(2,1)S(1)} %collective-permute-done.37.refs_7_), channel_id=1, source_target_pairs={{0,8},{8,0},{16,24},{24,16},{1,9},{9,1},{17,25},{25,17},{2,10},{10... | collective-permute-start | bytes 3145736 | tf_op jit(solution)/shard_map/ppermute | solution.py:555
  363.2 35.0 %collective-permute-start.39 = (f16[16,136,128]{2,1,0:T(8,128)(2,1)S(1)}, f16[16,136,128]{2,1,0:T(8,128)(2,1)S(1)}, u32[]{:S(2)}, u32[]{:S(2)}) collective-permute-start(f16[16,136,128]{2,1,0:T(8,128)(2,1)S(1)} %convert_element_type.92), channel_id=1, source_target_pairs={{0,16},{8,24},{16,0},{24,8},{1,17},{9,25},{17,1},{25,9},{2,18},{10... | collective-permute-start | bytes 1671176 | tf_op jit(solution)/shard_map/ppermute | solution.py:559
  378.2 46.9 %collective-permute-start.42 = (bf16[1024,512]{1,0:T(8,128)(2,1)}, bf16[1024,512]{1,0:T(8,128)(2,1)S(1)}, u32[]{:S(2)}, u32[]{:S(2)}) collective-permute-start(bf16[1024,512]{1,0:T(8,128)(2,1)} %collective-permute-done.41.refs_7_), channel_id=1, source_target_pairs={{0,8},{8,0},{16,24},{24,16},{1,9},{9,1},{17,25},{25,17},{2,10},{10... | collective-permute-start | bytes 3145736 | tf_op jit(solution)/shard_map/ppermute | solution.py:555
  397.8 39.9 %collective-permute-start.36 = (bf16[1024,512]{1,0:T(8,128)(2,1)S(1)}, bf16[1024,512]{1,0:T(8,128)(2,1)S(1)}, u32[]{:S(2)}, u32[]{:S(2)}) collective-permute-start(bf16[1024,512]{1,0:T(8,128)(2,1)S(1)} %collective-permute-done.35.refs_7_), channel_id=1, source_target_pairs={{0,8},{8,0},{16,24},{24,16},{1,9},{9,1},{17,25},{25,17},{2,10},{10... | collective-permute-start | bytes 3145736 | tf_op jit(solution)/shard_map/ppermute | solution.py:555
  398.4 14.7 %collective-permute-start.43 = (f16[16,136,128]{2,1,0:T(8,128)(2,1)S(1)}, f16[16,136,128]{2,1,0:T(8,128)(2,1)S(1)}, u32[]{:S(2)}, u32[]{:S(2)}) collective-permute-start(f16[16,136,128]{2,1,0:T(8,128)(2,1)S(1)} %convert_element_type.96), channel_id=1, source_target_pairs={{0,16},{8,24},{16,0},{24,8},{1,17},{9,25},{17,1},{25,9},{2,18},{10... | collective-permute-start | bytes 1671176 | tf_op jit(solution)/shard_map/ppermute | solution.py:559
  398.5 1.2 copy-start.8
  411.4 13.6 %collective-permute-start.40 = (f16[16,136,128]{2,1,0:T(8,128)(2,1)S(1)}, f16[16,136,128]{2,1,0:T(8,128)(2,1)S(1)}, u32[]{:S(2)}, u32[]{:S(2)}) collective-permute-start(f16[16,136,128]{2,1,0:T(8,128)(2,1)S(1)} %convert_element_type.94), channel_id=1, source_target_pairs={{0,16},{8,24},{16,0},{24,8},{1,17},{9,25},{17,1},{25,9},{2,18},{10... | collective-permute-start | bytes 1671176 | tf_op jit(solution)/shard_map/ppermute | solution.py:559
  437.1 15.6 %collective-permute-start.45 = (f16[16,136,128]{2,1,0:T(8,128)(2,1)S(1)}, f16[16,136,128]{2,1,0:T(8,128)(2,1)S(1)}, u32[]{:S(2)}, u32[]{:S(2)}) collective-permute-start(f16[16,136,128]{2,1,0:T(8,128)(2,1)S(1)} %convert_element_type.100), channel_id=1, source_target_pairs={{0,16},{8,24},{16,0},{24,8},{1,17},{9,25},{17,1},{25,9},{2,18},{10... | collective-permute-start | bytes 1671176 | tf_op jit(solution)/shard_map/ppermute | solution.py:559
  441.4 19.9 %collective-permute-start.44 = (f16[16,136,128]{2,1,0:T(8,128)(2,1)S(1)}, f16[16,136,128]{2,1,0:T(8,128)(2,1)S(1)}, u32[]{:S(2)}, u32[]{:S(2)}) collective-permute-start(f16[16,136,128]{2,1,0:T(8,128)(2,1)S(1)} %convert_element_type.98), channel_id=1, source_target_pairs={{0,16},{8,24},{16,0},{24,8},{1,17},{9,25},{17,1},{25,9},{2,18},{10... | collective-permute-start | bytes 1671176 | tf_op jit(solution)/shard_map/ppermute | solution.py:559

commit v2 on v0

v2 whole, which is shorter than its diff:
```python
import functools

import jax
import jax.numpy as jnp
from jax import lax
from jax.experimental import pallas as pl
from jax.experimental.pallas import tpu as pltpu
from jax.sharding import PartitionSpec as P

BLOCK = 128
REACH = 56
CHUNK = 4
WINDOW = 16
PARTS = 8
ROOM = 60
UNROLL = 4
CODED = BLOCK + 8
SEEN = {4: (0,), 6: (1,)}
COSTS = (10000, 10000, 10000, 10000, 500, 10000, 500)
TOP = 10.0
F32 = jnp.float32
BF16 = jnp.bfloat16
ANY = pl.BlockSpec(memory_space=pl.ANY)
SMEM = pl.BlockSpec(memory_space=pltpu.SMEM)
VMEM = pl.BlockSpec(memory_space=pltpu.VMEM)


def params(mib):
    return pltpu.CompilerParams(vmem_limit_bytes=mib << 20)


def from_behind(value, axis, steps):
    count = lax.axis_size(axis)
    first, last = (max(0, -steps), min(count, count - steps))
    return lax.ppermute(value, axis, [(source, source + steps) for source in range(first, last)])


def plain_shards(yields, partners):
    snaps_local, columns = yields.shape
    blocks_local = columns // BLOCK
    total_snaps = snaps_local * lax.axis_size("snap")
    local_sums = jnp.sum(yields, axis=0, dtype=F32)
    totals = lax.psum(local_sums, "snap")
    bond_means = totals / total_snaps
    centered = (yields.astype(F32) - bond_means[None, :]).astype(BF16)
    extent = blocks_local + REACH - 1
    hop_count = (extent - 1) // blocks_local
    pieces = [centered]
    for distance in range(1, hop_count + 1):
        kept_blocks = min(blocks_local, extent - distance * blocks_local)
        kept_cols = kept_blocks * BLOCK
        pieces.append(from_behind(centered[:, :kept_cols], "bond", -distance))
    extended = jnp.concatenate(pieces, axis=1).reshape(snaps_local, -1, BLOCK)
    ext_blocks = extended.shape[1]
    first_block = lax.axis_index("bond") * blocks_local
    live_all = partners >= 0
    index_all = jnp.clip(jnp.where(live_all, partners - first_block, 0), 0, ext_blocks - 1)
    inverse = 1.0 / (total_snaps - 1)

    def block_tiles(args):
        block_row, index_row, live_row = args
        own_block = lax.dynamic_index_in_dim(extended, block_row, 1, keepdims=False)
        chosen = jnp.take(extended, index_row, axis=1)
        tile_sum = jnp.einsum("sa,scb->cab", own_block, chosen, preferred_element_type=F32)
        return tile_sum * (live_row.astype(F32) * inverse)[:, None, None]

    per_block = lax.map(
        block_tiles, (jnp.arange(blocks_local, dtype=jnp.int32), index_all, live_all)
    )
    covariance_tiles = lax.psum_scatter(
        jnp.transpose(per_block, (1, 0, 2, 3)), "snap", scatter_dimension=0, tiled=True
    )
    return (bond_means, covariance_tiles)


def cost(micros):
    return pl.CostEstimate(flops=int(micros * 1e9), bytes_accessed=int(micros * 3e6), transcendentals=0)


def token():
    return jax.ShapeDtypeStruct((8, BLOCK), F32)


def feed_kernel(bounds, plan, odd_ref, yields, far, *refs):
    buffers, (in_sems, out_sems) = refs[-2 - len(plan):-2], refs[-2:]
    outs = refs[-3 - 2 * len(plan):-3 - len(plan)]
    odd = odd_ref[0]
    parts = in_sems.shape[1]
    pieces = [(n, r) for r in range(parts) for n in range(len(plan))]

    def span(ref, r):
        rows = ref.shape[0] // parts
        return pl.ds(r * rows, rows)

    def fetch(src, first, n, r):
        rows, wide = span(src, r), buffers[n].shape[1]
        part = src.at[rows, pl.ds(first * BLOCK, wide)]
        return pltpu.make_async_copy(part, buffers[n].at[rows], in_sems.at[n, r])

    def own(n, r):
        return fetch(yields, bounds[plan[n][1]], n, r)

    def relayed(n, r):
        return fetch(far, 0, n, r)

    def store(n, r):
        rows = span(yields, r)
        return pltpu.make_async_copy(buffers[n].at[rows], outs[n].at[rows], out_sems.at[n, r])

    for n, r in pieces:
        if plan[n][0] == "own":
            own(n, r).start()
        else:
            pl.when(odd == 1)(lambda: own(n, r).start())
            pl.when(odd == 0)(lambda: relayed(n, r).start())
    for n, r in pieces:
        own(n, r).wait()
        store(n, r).start()
    for n, r in pieces:
        store(n, r).wait()


def feed(cfg, plan, odd, yields, far, *tokens):
    bounds, parts = cfg["bounds"], 4
    shapes = [(yields.shape[0], (bounds[t + 1] - bounds[t]) * BLOCK) for _, t in plan]
    return pl.pallas_call(
        functools.partial(feed_kernel, bounds, plan),
        in_specs=[SMEM] + [ANY] * (2 + len(tokens)),
        out_specs=[ANY] * (len(plan) + 1),
        out_shape=[jax.ShapeDtypeStruct(shape, BF16) for shape in shapes] + [token()],
        scratch_shapes=[pltpu.VMEM(shape, BF16) for shape in shapes]
        + [pltpu.SemaphoreType.DMA((len(plan), parts))] * 2,
        compiler_params=params(ROOM),
        cost_estimate=cost(COSTS[0]),
        name="feed",
    )(odd, yields, far, *tokens)


def rest_kernel(_, out):
    pass


def rest(after):
    return pl.pallas_call(
        rest_kernel,
        in_specs=[ANY],
        out_specs=ANY,
        out_shape=token(),
        compiler_params=params(ROOM),
        cost_estimate=cost(COSTS[0]),
        name="rest",
    )(after)


def sums_kernel(raw_ref, _, out_ref):
    out_ref[0] = jnp.sum(raw_ref[...].astype(F32), axis=0, keepdims=True)


def column_sums(yields, after):
    snaps, columns = yields.shape
    wide = 4 * BLOCK
    steps = columns // wide
    return pl.pallas_call(
        sums_kernel,
        grid=(steps,),
        in_specs=[pl.BlockSpec((snaps, wide), lambda i: (0, i)), ANY],
        out_specs=pl.BlockSpec((1, 1, wide), lambda i: (i, 0, 0)),
        out_shape=jax.ShapeDtypeStruct((steps, 1, wide), F32),
        compiler_params=params(ROOM),
        cost_estimate=cost(COSTS[1]),
        name="column_sums",
    )(yields, after).reshape(columns)


def transpose_kernel(group, raw_ref, mean_ref, out_ref):
    for g in range(group):
        cols = pl.ds(g * BLOCK, BLOCK)
        block = raw_ref[:, cols].astype(F32) - mean_ref[0, :, cols]
        out_ref[g] = block.T.astype(BF16)


def centered_transposed(yields, means):
    snaps, columns = yields.shape
    group = 2
    blocks = columns // BLOCK
    steps = blocks // group
    return pl.pallas_call(
        functools.partial(transpose_kernel, group),
        grid=(steps,),
        in_specs=[
            pl.BlockSpec((snaps, group * BLOCK), lambda i: (0, i)),
            pl.BlockSpec((1, 1, group * BLOCK), lambda i: (i, 0, 0)),
        ],
        out_specs=pl.BlockSpec((group, BLOCK, snaps), lambda i: (i, 0, 0)),
        out_shape=jax.ShapeDtypeStruct((blocks, BLOCK, snaps), BF16),
        compiler_params=params(ROOM),
        cost_estimate=cost(COSTS[2]),
        name="center_transpose",
    )(yields, means.reshape(steps, 1, group * BLOCK))


def entry(entries, n):
    v = entries[n]
    return (v >> 12) & 63, (v >> 8) & 15, v & 255


def travels(entries, n):
    return (entries[n] >> 18) & 1 == 1


def output_place(entries, out, n):
    row, slot, _ = entry(entries, n)
    return out.at[slot, row]


def all_rows(xa, xb, rows_a, rows_b, sems):
    rows = xa.shape[0] // PARTS

    def copies(part):
        span = pl.ds(part * rows, rows)
        return (
            pltpu.make_async_copy(xa.at[span], rows_a.at[span], sems.at[0, part]),
            pltpu.make_async_copy(xb.at[span], rows_b.at[span], sems.at[1, part]),
        )

    def start():
        for part in reversed(range(PARTS)):
            for copy in copies(part):
                copy.start()

    def wait_down_to(here, need):
        for part in reversed(range(PARTS)):

            @pl.when((here > part) & (need <= part))
            def _():
                for copy in copies(part):
                    copy.wait()

        return jnp.minimum(here, need)

    def begin(g, wanted):
        pass

    def ready(g, here, wanted):
        lowest = functools.reduce(jnp.minimum, wanted)
        need = sum(((lowest >= part * rows).astype(jnp.int32) for part in range(1, PARTS)), 0)
        return wait_down_to(here, need)

    def finish(here):
        wait_down_to(here, 0)

    return start, (begin, ready, finish)


def few_rows(xa, xb, rows_a, rows_b, sems):
    def copies(g, wanted):
        for u, row in enumerate(wanted):
            at = (g & 1) * UNROLL + u
            yield pltpu.make_async_copy(xa.at[row], rows_a.at[at], sems.at[0, at])
            yield pltpu.make_async_copy(xb.at[row], rows_b.at[at], sems.at[1, at])

    def begin(g, wanted):
        for copy in copies(g, wanted):
            copy.start()

    def ready(g, here, wanted):
        for copy in copies(g, wanted):
            copy.wait()
        return here

    def finish(here):
        pass

    return begin, ready, finish


def tile_loop(cfg, step, info, work, out, send, stage, store_sem, rows_in, product):
    lo = info[cfg["cut_o"] + step] + info[cfg["cut_m"] + step]
    hi = info[cfg["cut_o"] + step + 1] + info[cfg["cut_m"] + step + 1]
    groups = lax.div(hi - lo + UNROLL - 1, UNROLL)
    begin, ready, finish = rows_in

    def rows_of(g):
        return [entry(work, lo + g * UNROLL + u)[0] for u in range(UNROLL)]

    def each_store(g, act):
        for u in range(UNROLL):
            n, at = lo + g * UNROLL + u, (g & 1) * UNROLL + u
            away = travels(work, n)

            @pl.when((n < hi) & away)
            def _():
                dst = send.at[work[n] >> 19]
                act(pltpu.make_async_copy(stage.at[at], dst, store_sem.at[at]))

            @pl.when((n < hi) & jnp.logical_not(away))
            def _():
                src, dst = stage.at[at, pl.ds(0, BLOCK)], output_place(work, out, n)
                act(pltpu.make_async_copy(src, dst, store_sem.at[at]))

    pl.when(groups > 0)(lambda: begin(0, rows_of(0)))

    def body(g, here):
        base = lo + g * UNROLL
        found = [entry(work, base + u) for u in range(UNROLL)]
        pl.when(g + 1 < groups)(lambda: begin(g + 1, rows_of(g + 1)))
        here = ready(g, here, [row for row, _, _ in found])
        pl.when(g >= 2)(lambda: each_store(g - 2, lambda copy: copy.wait()))
        values = [
            product((g & 1) * UNROLL + u, row, rel) for u, (row, _, rel) in enumerate(found)
        ]
        for u in range(UNROLL):
            at = (g & 1) * UNROLL + u
            top = jnp.maximum(jnp.max(jnp.abs(values[u]), axis=0, keepdims=True), 1e-30)
            power = jnp.where(travels(work, base + u), TOP - jnp.ceil(jnp.log2(top)), 0.0)
            stage[at, 0:BLOCK] = values[u] * jnp.exp2(power)
            stage[at, BLOCK:CODED] = jnp.broadcast_to(power, (CODED - BLOCK, BLOCK))
        each_store(g, lambda copy: copy.start())
        return here

    finish(lax.fori_loop(0, groups, body, jnp.int32(PARTS)))
    pl.when(groups >= 2)(lambda: each_store(groups - 2, lambda copy: copy.wait()))
    pl.when(groups >= 1)(lambda: each_store(groups - 1, lambda copy: copy.wait()))


def send_window(info, at, send, window, sem):
    copy = pltpu.make_async_copy(send.at[pl.ds(info[at], window.shape[0])], window, sem)
    copy.start()
    copy.wait()


def stage_scratch(xa, rows):
    return [
        pltpu.VMEM((rows,) + xa.shape[1:], BF16),
        pltpu.VMEM((rows,) + xa.shape[1:], BF16),
        pltpu.VMEM((2 * UNROLL, CODED, BLOCK), F32),
        pltpu.SemaphoreType.DMA((2, max(PARTS, 2 * UNROLL))),
        pltpu.SemaphoreType.DMA((2 * UNROLL,)),
        pltpu.SemaphoreType.DMA,
    ]


def own_kernel(cfg, info, mlist, work, means, xa, xb, *refs):
    means_out, refs = refs[-13], refs[-12:]
    means_out[...] = means[...]
    out, send, window, _, rows_a, rows_b, stage, row_sem, store_sem, sem, zero, zero_sem = refs
    start_rows, rows_in = all_rows(xa, xb, rows_a, rows_b, row_sem)
    start_rows()

    def product(at, row, rel):
        p = jnp.minimum(rel, xa.shape[0] - 1)
        dims = (((1,), (1,)), ((), ()))
        acc = lax.dot_general(rows_a[row], rows_a[p], dims, preferred_element_type=F32)
        acc += lax.dot_general(rows_b[row], rows_b[p], dims, preferred_element_type=F32)
        return acc * cfg["inverse"]

    zero[...] = jnp.zeros_like(zero)

    def clear(n):
        return pltpu.make_async_copy(zero, output_place(mlist, out, n), zero_sem)

    def start_clear(n, carry):
        clear(n).start()
        return carry

    def wait_clear(n, carry):
        clear(n).wait()
        return carry

    live = info[cfg["cut_m"] + cfg["stages"]]
    tile_loop(cfg, 0, info, work, out, send, stage, store_sem, rows_in, product)
    lax.fori_loop(live, cfg["entries"], start_clear, 0)
    send_window(info, cfg["win_o"], send, window, sem)
    lax.fori_loop(live, cfg["entries"], wait_clear, 0)


def own_stage(cfg, info, mlist, work, means, xa, xb, *after):
    blocks = xa.shape[0]
    room = max(cfg["windows"] + (WINDOW,))
    return pl.pallas_call(
        functools.partial(own_kernel, cfg),
        in_specs=[SMEM] * 3 + [VMEM] + [ANY] * (2 + len(after)),
        out_specs=[VMEM, ANY, ANY, VMEM, ANY],
        out_shape=[
            jax.ShapeDtypeStruct(means.shape, F32),
            jax.ShapeDtypeStruct((cfg["slots"], blocks, BLOCK, BLOCK), F32),
            jax.ShapeDtypeStruct((cfg["entries"] + room, CODED, BLOCK), F32),
            jax.ShapeDtypeStruct((cfg["windows"][0], CODED, BLOCK), F32),
            token(),
        ],
        scratch_shapes=stage_scratch(xa, blocks)
        + [pltpu.VMEM((BLOCK, BLOCK), F32), pltpu.SemaphoreType.DMA],
        compiler_params=params(ROOM),
        cost_estimate=cost(COSTS[3]),
        name="own_tiles",
    )(info, mlist, work, means, xa, xb, *after)


def merge_parts(cfg, lo, count, mlist, arrived, out, mine, theirs, mine_sem, theirs_sem):
    def read_mine(r):
        src = output_place(mlist, out, lo + r)
        return pltpu.make_async_copy(src, mine.at[r], mine_sem.at[r])

    def read_theirs(r):
        return pltpu.make_async_copy(arrived.at[r], theirs.at[r], theirs_sem.at[r])

    def write(r):
        dst = output_place(mlist, out, lo + r)
        return pltpu.make_async_copy(mine.at[r], dst, mine_sem.at[r])

    def first(r, carry):
        read_mine(r).start()
        read_theirs(r).start()
        return carry

    def second(r, carry):
        read_mine(r).wait()
        read_theirs(r).wait()
        scale = jnp.exp2(-theirs[r, BLOCK:BLOCK + 1])
        mine[r] = mine[r] + theirs[r, 0:BLOCK] * scale
        write(r).start()
        return carry

    def third(r, carry):
        write(r).wait()
        return carry

    return tuple(
        lambda step=step: lax.fori_loop(0, count, step, 0) for step in (first, second, third)
    )


def merge_scratch(size):
    return [
        pltpu.VMEM((size, BLOCK, BLOCK), F32),
        pltpu.VMEM((size, CODED, BLOCK), F32),
        pltpu.SemaphoreType.DMA((size,)),
        pltpu.SemaphoreType.DMA((size,)),
    ]


def join_kernel(spans, *refs):
    kinds = 2 if len(spans) > 0 and any(kind for kind, _, _ in spans) else 1
    means, refs = refs[:kinds], refs[kinds:]
    raw = refs[:len(spans)]
    out, _, rawbuf, done, raw_sem, out_sem = refs[-6:]
    places = [(n, kind, first, j) for n, (kind, first, w) in enumerate(spans) for j in range(w)]

    def fetch(at):
        n, _, _, j = places[at]
        src = raw[n].at[:, pl.ds(j * BLOCK, BLOCK)]
        return pltpu.make_async_copy(src, rawbuf.at[at], raw_sem.at[at])

    def store(at):
        return pltpu.make_async_copy(done.at[at], out.at[at], out_sem.at[at])

    for at in range(len(places)):
        fetch(at).start()
    for at, (_, kind, first, j) in enumerate(places):
        fetch(at).wait()
        block = rawbuf[at].astype(F32) - means[kind][first + j:first + j + 1, :]
        done[at] = block.astype(BF16)
        store(at).start()
    for at in range(len(places)):
        store(at).wait()


def join(means, raw, spans, *after):
    snaps = raw[0].shape[0]
    kinds = 2 if any(kind for kind, _, _ in spans) else 1
    blocks = (sum(w for _, _, w in spans), snaps, BLOCK)
    return pl.pallas_call(
        functools.partial(join_kernel, spans),
        in_specs=[VMEM] * kinds + [ANY] * (len(raw) + len(after)),
        out_specs=[ANY, ANY],
        out_shape=[jax.ShapeDtypeStruct(blocks, BF16), token()],
        scratch_shapes=[
            pltpu.VMEM(blocks, BF16),
            pltpu.VMEM(blocks, BF16),
            pltpu.SemaphoreType.DMA((blocks[0],)),
            pltpu.SemaphoreType.DMA((blocks[0],)),
        ],
        compiler_params=params(ROOM),
        cost_estimate=cost(COSTS[4]),
        name="center_join",
    )(*means[:kinds], *raw, *after)


def halo_kernel(cfg, step, merges, *refs):
    info, mlist, work, cast, xa, xb = refs[:6]
    ca, cb = refs[6:8]
    refs = refs[8:]
    blocks = cfg["blocks"]
    first_block, end_block = cfg["spans"][step - 1]
    arrived, rest = refs[:len(merges)], refs[len(merges):]
    out, send, _, vote = rest[3:7]
    rest = rest[7:]
    if cfg["windows"][step]:
        window, rest = rest[0], rest[1:]
    rows_a, rows_b, stage, row_sem, store_sem, sem, ya, yb, raw_sem = rest[:9]
    vote[0] = cast[0]
    rows_in = few_rows(xa, xb, rows_a, rows_b, row_sem)
    halves = [
        pltpu.make_async_copy(src, dst, raw_sem.at[n])
        for n, (src, dst) in enumerate(((ca, ya), (cb, yb)))
    ]
    for copy in halves:
        copy.start()
    parts = []
    for n, w in enumerate(merges):
        lo = info[cfg["win_m"] + w]
        count = info[cfg["win_m"] + w + 1] - lo
        parts.append(merge_parts(cfg, lo, count, mlist, arrived[n], out, *rest[9 + 4 * n:13 + 4 * n]))
    for first, _, _ in parts:
        first()
    for copy in halves:
        copy.wait()

    def product(at, row, rel):
        near = rel - blocks - first_block
        far = rel - 2 * blocks - first_block + end_block - first_block
        j = jnp.clip(jnp.where(rel >= 2 * blocks, far, near), 0, ya.shape[0] - 1)
        acc = jnp.dot(rows_a[at], ya[j], preferred_element_type=F32)
        acc += jnp.dot(rows_b[at], yb[j], preferred_element_type=F32)
        return acc * cfg["inverse"]

    tile_loop(cfg, step, info, work, out, send, stage, store_sem, rows_in, product)
    for _, second, _ in parts:
        second()
    if cfg["windows"][step]:
        send_window(info, cfg["win_o"] + step, send, window, sem)
    for _, _, third in parts:
        third()


def halo_stage(cfg, step, merges, info, mlist, work, cast, xa, xb, halves, arrived, out, send, after):
    count = 6 + len(halves) + len(arrived)
    size = cfg["windows"][step]
    shapes = [
        jax.ShapeDtypeStruct(out.shape, F32),
        jax.ShapeDtypeStruct(send.shape, F32),
        token(),
        jax.ShapeDtypeStruct((1,), jnp.int32),
        jax.ShapeDtypeStruct((size, CODED, BLOCK), F32),
    ]
    scratch = stage_scratch(xa, 2 * UNROLL) + [
        pltpu.VMEM(halves[0].shape[-3:], BF16),
        pltpu.VMEM(halves[0].shape[-3:], BF16),
        pltpu.SemaphoreType.DMA((2,)),
    ]
    for window in arrived:
        scratch += merge_scratch(window.shape[0])
    made = pl.pallas_call(
        functools.partial(halo_kernel, cfg, step, merges),
        in_specs=[SMEM] * 4 + [ANY] * (count - 1),
        out_specs=[ANY, ANY, ANY, SMEM, VMEM][:5 if size else 4],
        out_shape=shapes[:5 if size else 4],
        scratch_shapes=scratch,
        input_output_aliases={count: 0, count + 1: 1},
        compiler_params=params(ROOM),
        cost_estimate=cost(COSTS[5]),
        name="halo_tiles",
    )(info, mlist, work, cast, xa, xb, *halves, *arrived, out, send, after)
    return made if size else (*made, None)


def merge_kernel(cfg, span, mlist, arrived, _, out, *scratch):
    lo = span[0]
    for part in merge_parts(cfg, lo, span[1] - lo, mlist, arrived, out, *scratch):
        part()


def merge(cfg, span, mlist, arrived, out):
    return pl.pallas_call(
        functools.partial(merge_kernel, cfg),
        in_specs=[SMEM, SMEM, ANY, ANY],
        out_specs=ANY,
        out_shape=jax.ShapeDtypeStruct(out.shape, F32),
        scratch_shapes=merge_scratch(arrived.shape[0]),
        input_output_aliases={3: 0},
        compiler_params=params(ROOM),
        cost_estimate=cost(COSTS[6]),
        name="merge_tiles",
    )(span, mlist, arrived, out)


def work_list(value, stage):
    entries = value.size
    ids = jnp.arange(entries, dtype=jnp.int32)
    key = (stage + 1) * entries - ids
    rank = jnp.sum((key[None, :] < key[:, None]).astype(jnp.int32), axis=1).astype(jnp.int32)
    ordered = jnp.sum(jnp.where(rank[None, :] == ids[:, None], value[None, :], 0), axis=1)
    return jnp.pad(ordered.astype(jnp.int32), (0, UNROLL)), rank


def window_starts(cuts, sizes):
    sent = jnp.array([sum(sizes[:w]) for w in range(len(sizes) + 1)], jnp.int32)
    later = sent[:, None] - sent[None, :]
    reach = jnp.where(later >= 0, cuts[..., None, :] + later, jnp.int32(1 << 30))
    return jnp.min(reach, axis=-1).astype(jnp.int32)


def hop_plan(blocks):
    hops = blocks // CHUNK
    stages = [(t, t + 1) for t in range(0, hops - 2, 2)] + [(hops - 2,), (hops - 1,)]
    return tuple(range(0, blocks + 1, CHUNK)), tuple(stages)


def paired_shards(yields, partners):
    snaps_local, columns = yields.shape
    blocks = columns // BLOCK
    snap_count, bond_count = lax.axis_size("snap"), lax.axis_size("bond")
    total_snaps = snaps_local * snap_count
    q, d = lax.axis_index("snap"), lax.axis_index("bond")
    odd = lax.rem(d, 2).astype(jnp.int32)[None]
    slots = partners.shape[1] // snap_count
    bounds, takes = hop_plan(blocks)
    hops = len(bounds) - 1
    far_blocks = REACH - 1 - blocks
    stages = len(takes) + 1
    windows = (3 * WINDOW,) + (2 * WINDOW,) * (stages - 4) + (0, WINDOW + 8, WINDOW + 4)
    cfg = {
        "entries": blocks * slots,
        "spans": tuple((bounds[hop[0]], bounds[hop[-1] + 1]) for hop in takes),
        "slots": slots,
        "blocks": blocks,
        "bounds": bounds,
        "windows": windows,
        "stages": stages,
        "cut_m": 0,
        "cut_o": stages + 1,
        "win_o": 2 * (stages + 1),
        "win_m": 3 * (stages + 1),
        "inverse": 1.0 / (total_snaps - 1),
    }

    def other_core(value):
        return lax.ppermute(value, "snap", [(s, s ^ 1) for s in range(snap_count)])

    def across(value):
        return lax.ppermute(value, "snap", [(s, s ^ 2) for s in range(snap_count)])

    def other_chip(value):
        return across(value.astype(jnp.float16)).astype(F32)

    far, near = [None] * hops, [None] * hops

    def send_far(t, value):
        far[t] = lax.ppermute(value, "bond", [(s, s - 2) for s in range(2, bond_count)])

    def send_near(t, value):
        near[t] = lax.ppermute(value, "bond", [(s, s ^ 1) for s in range(bond_count)])

    second, mark = feed(cfg, (("own", 1),), odd, yields, yields)
    send_far(1, second)
    first, mark = feed(cfg, (("own", 0),), odd, yields, yields, mark)
    send_far(0, first)

    def step(t, *marks):
        plan = (("pick", t),)
        if t < hops - 2:
            plan += (("own", t + 2),)
        made = feed(cfg, plan, odd, yields, far[t], *marks)
        send_near(t, made[0])
        if len(plan) == 2:
            send_far(t + 2, made[1])
        return made[-1]

    sums = column_sums(yields, mark)
    sums = sums + other_core(sums)
    totals = sums + across(sums)
    bond_means = totals / total_snaps
    xa = centered_transposed(yields, bond_means)
    xb = other_core(xa)

    rel = partners - d * blocks
    live = partners >= 0
    halo_block = jnp.where(rel < 2 * blocks, rel - blocks, rel - 2 * blocks)
    ends = jnp.array([end for _, end in cfg["spans"][:-1]], jnp.int32)
    taken = jnp.sum((halo_block[..., None] >= ends).astype(jnp.int32), axis=-1)
    stage = jnp.where(live, jnp.where(rel < blocks, 0, taken + 1), stages)
    groups = stage.reshape(blocks, snap_count, slots)
    marks = jnp.arange(stages + 1, dtype=jnp.int32)
    cuts = jnp.sum((groups[..., None] < marks).astype(jnp.int32), axis=(0, 2))
    starts = window_starts(cuts, windows)
    left = jnp.max(cuts[:, -1] - starts[:, -1])

    def row_of(table, owner):
        return lax.dynamic_index_in_dim(table, owner, 0, keepdims=False)

    def listed(owner):
        def cut(a):
            return lax.dynamic_slice_in_dim(a, owner * slots, slots, axis=1)

        rows = lax.broadcasted_iota(jnp.int32, (blocks, slots), 0)
        value = rows * 4096 + lax.broadcasted_iota(jnp.int32, (blocks, slots), 1) * 256
        value, when = value + cut(jnp.where(live, rel, 0)), cut(stage)
        ordered, rank = work_list(value.reshape(-1), when.reshape(-1))
        return value, when, ordered, rank.reshape(blocks, slots)

    mvalue, mstage, mlist, _ = listed(q)
    ovalue, ostage, _, orank = listed(q ^ 2)
    ovalue = ovalue + (2 * orank + 1) * (1 << 18)
    work, _ = work_list(
        jnp.concatenate([ovalue, mvalue], axis=1).reshape(-1),
        jnp.concatenate([ostage, mstage], axis=1).reshape(-1),
    )
    mcuts, mwin, owin = row_of(cuts, q), row_of(starts, q), row_of(starts, q ^ 2)
    info = jnp.concatenate([mcuts, row_of(cuts, q ^ 2), owin, mwin])
    vote = left.astype(jnp.int32)[None]

    def center(group, *marks):
        raw, spans = [], []
        for kind, came, limit in ((0, near, blocks), (1, far, far_blocks)):
            for t in takes[group]:
                if bounds[t] < limit:
                    raw.append(came[t])
                    spans.append((kind, bounds[t], bounds[t + 1] - bounds[t]))
        mine, mark = join((near_mean, far_mean), raw, tuple(spans), *marks)
        return (mine, other_core(mine)), mark

    mark = step(0, mark)
    block_means = bond_means.reshape(blocks, BLOCK)
    block_means, out, send, window, mark = own_stage(
        cfg, info, mlist, work, block_means, xa, xb, mark
    )
    near_mean = from_behind(block_means, "bond", -1)
    far_mean = from_behind(block_means, "bond", -2)
    arrived = {0: other_chip(window)}
    mark = step(1, mark)
    fed, merged = 2, 0
    for group, hop in enumerate(takes):
        while fed < hops and fed <= hop[-1] + 1:
            mark = step(fed, mark, *[arrived[w] for w in SEEN.get(fed, ())])
            fed += 1
        last = group + 1 == len(takes)
        halves, mark = center(group, mark, *([arrived[max(arrived)]] if last else []))
        if fed < hops and len(hop) == 2:
            mark = step(fed, mark, *[arrived[w] for w in SEEN.get(fed, ())])
            fed += 1
        elif last:
            mark = rest(mark)
        merges = tuple(w for w in sorted(arrived) if merged <= w < group or (last and w >= merged))
        merged = max((*merges, merged - 1)) + 1
        out, send, mark, vote, window = halo_stage(
            cfg, group + 1, merges, info, mlist, work, vote, xa, xb, halves,
            [arrived[w] for w in merges], out, send, mark,
        )
        if window is not None:
            arrived[group + 1] = other_chip(window)
    for stride in range((bond_count - 1).bit_length()):
        pairs = [(s, s ^ (1 << stride)) for s in range(bond_count)]
        vote = jnp.maximum(vote, lax.ppermute(vote, "bond", pairs))
    out = merge(cfg, mwin[-2:], mlist, arrived[len(takes)], out)

    trips = (vote[0] + WINDOW - 1) // WINDOW

    def more(state):
        return state[0] < trips

    def turn(state):
        trip, result = state
        at = jnp.minimum(owin[-1] + trip * WINDOW, send.shape[0] - WINDOW)
        got = other_chip(lax.dynamic_slice_in_dim(send, at, WINDOW, axis=0))
        lo = jnp.minimum(mwin[-1] + trip * WINDOW, mcuts[-1])
        hi = jnp.minimum(lo + WINDOW, mcuts[-1])
        return trip + 1, merge(cfg, jnp.stack([lo, hi]), mlist, got, result)

    _, out = lax.while_loop(more, turn, (jnp.int32(0), out))
    return (bond_means, out)


def shards(yields, partners):
    blocks = yields.shape[1] // BLOCK
    snap_count, bond_count = lax.axis_size("snap"), lax.axis_size("bond")
    two_hops = blocks < REACH - 1 <= 2 * blocks
    if (
        two_hops
        and snap_count == 4
        and bond_count & (bond_count - 1) == 0
        and blocks % (2 * CHUNK) == 0
        and blocks // CHUNK >= 4
        and blocks <= 64
        and partners.shape[1] <= 64
        and blocks % PARTS == 0
        and partners.shape[1] % snap_count == 0
        and yields.shape[0] % BLOCK == 0
    ):
        return paired_shards(yields, partners)
    return plain_shards(yields, partners)


def solution(mesh):
    return jax.shard_map(
        shards,
        mesh=mesh,
        in_specs=(P("snap", "bond"), P("bond", None)),
        out_specs=(P("bond"), P("snap", "bond", None, None)),
        check_vma=False,
    )
```

time: 1250 us -> 332 us (0.27)
  waiting for transfers between devices: 533 us -> 56.1 us
  local copies, waits for them, and re-layouts: 449 us -> 6.26 us
  Pallas kernels: 0 us -> 168 us
  matrix products: 124 us -> 0 us
  loops' own time: 63.4 us -> 0.01 us
  starting transfers between devices: 8.32 us -> 67.9 us
  other arithmetic: 42.8 us -> 24.3 us
    gather x32 -> x0, local copies, waits for them, and re-layouts: 339 us -> none  [block_tiles(): chosen = jnp.take(extended, index_row, axis=1)]
    ppermute x2, waiting for transfers between devices: 297 us -> 0.01 us  [from_behind(): lax.ppermute(value, axis, [(source, source + steps) for source in range(f...]
    reduce_scatter x1 -> x0, waiting for transfers between devices: 236 us -> none  [shards(): lax.psum_scatter(jnp.transpose(per_block, (1, 0, 2, 3)), 'snap', scatter_...]
    pallas_call x0 -> x25, Pallas kernels: none -> 168 us  [the longest x5 75.8 us: halo_stage(): pl.pallas_call(functools.partial(halo_kernel, cfg, step, merges), in_spec...]
    dot_general x32 -> x0, matrix products: 124 us -> none  [block_tiles(): jnp.einsum('sa,scb->cab', own_block, chosen, preferred_element_type=jnp.f...]
    ppermute x0 -> x32, starting transfers between devices: none -> 64.1 us  [the longest x8 27.7 us: send_far(): lax.ppermute(value, 'bond', [(s, s - 2) for s in range(2, bond_count)])]
    another operation x1, loops' own time: 63.4 us -> 0.01 us  [paired_shards(): _, out = lax.while_loop(more, turn, (jnp.int32(0), out))]
    ppermute x0 -> x32, waiting for transfers between devices: none -> 56.1 us  [the longest x6 19.9 us: across(): return lax.ppermute(value, 'snap', [(s, s ^ 2) for s in range(snap_count)])]
  transfers between devices with their start and end apart: 3 -> 34, of which waited for: 2 -> 11; matrix products, arithmetic and copies ran while one was open for 0% -> 8% of each run, Pallas kernels for 0% -> 43%
where the time goes in v2:
time: 332 us; the launch traced here: 326 us
  Pallas kernels  168 us (51%)
  starting transfers between devices  67.9 us (20%)
  waiting for transfers between devices  56.1 us (17%)
  other arithmetic  24.3 us (7%)
  local copies, waits for them, and re-layouts  6.26 us (2%)
  between operations  3.77 us (1%)
    pallas_call x5, Pallas kernels, halo_stage(): pl.pallas_call(functools.partial(halo_kernel, cfg, step, merges), in_spec...  75.8 us
    ppermute x8, starting transfers between devices, send_far(): lax.ppermute(value, 'bond', [(s, s - 2) for s in range(2, bond_count)])  27.7 us
    pallas_call x1, Pallas kernels, own_stage(): pl.pallas_call(functools.partial(own_kernel, cfg), in_specs=[SMEM] * 3 +...  25.7 us
    pallas_call x10, Pallas kernels, feed(): pl.pallas_call(functools.partial(feed_kernel, bounds, plan), in_specs=[SM...  22.8 us
    pallas_call x5, Pallas kernels, join(): pl.pallas_call(functools.partial(join_kernel, spans), in_specs=[VMEM] * k...  20.5 us
    ppermute x8, starting transfers between devices, send_near(): lax.ppermute(value, 'bond', [(s, s ^ 1) for s in range(bond_count)])  20.3 us
    ppermute x6, waiting for transfers between devices, across(): return lax.ppermute(value, 'snap', [(s, s ^ 2) for s in range(snap_count)])  19.9 us
    convert_element_type x10, other arithmetic, other_chip(): return across(value.astype(jnp.float16)).astype(F32)  19.7 us
  transfers between devices with their start and end apart: 34, of which 11 were waited for; matrix products, arithmetic and copies ran while one was open for 8% of the time, Pallas kernels for 43%

profile of v2, /device:TPU:24, one launch (start us, length us, event | category | flops | bytes accessed | tf_op | source)
XLA Modules:
  0.0 326.0 jit_solution(5677182027223655046)
XLA Ops:
  0.6 2.0 feed.10
  2.7 2.0 feed.11
  4.7 6.9 %column_sums.1 = f32[8,1,512]{2,1,0:T(1,128)} custom-call(bf16[1024,4096]{1,0:T(8,128)(2,1)} %yields.19, f32[8,128]{1,0:T(8,128)} %get-tuple-element.110._.refs_0_), custom_call_target="tpu_custom_call" | custom-call | flops 9999999827968 | bytes 30000001024 | tf_op jit(solution)/shard_map/column_sums/pallas_call | solution.py:163
  11.6 3.4 %collective-permute-start.4 = (bf16[1024,512]{1,0:T(8,128)(2,1)}, bf16[1024,512]{1,0:T(8,128)(2,1)}, u32[]{:S(2)}, u32[]{:S(2)}) collective-permute-start(bf16[1024,512]{1,0:T(8,128)(2,1)} %get-tuple-element.111), channel_id=1, source_target_pairs={{2,0},{3,1},{4,2},{5,3},{6,4},{7,5},{10,8},{11,9},{12,10},{13,11},... | collective-permute-start | bytes 3145736 | tf_op jit(solution)/shard_map/ppermute | solution.py:649
  15.0 2.4 collective-permute-start.8
  21.1 0.8 fusion.4
  22.9 1.5 collective-permute-start.2
  27.3 13.2 %center_transpose.1.xa.refs_4_ = bf16[32,128,1024]{2,1,0:T(8,128)(2,1)} custom-call(bf16[1024,4096]{1,0:T(8,128)(2,1)} %yields.19, f32[16,1,256]{2,1,0:T(1,128)} %bitcast.27), custom_call_target="tpu_custom_call" | custom-call | flops 9999999827968 | bytes 30000001024 | tf_op jit(solution)/shard_map/center_transpose/pallas_call | solution.py:187
  40.6 2.4 feed.12
  43.0 1.6 collective-permute-start.7
  44.6 2.6 collective-permute-start.10
  47.1 6.9 %collective-permute-done.3.xb.refs_5_ = bf16[32,128,1024]{2,1,0:T(8,128)(2,1)} collective-permute-done((bf16[32,128,1024]{2,1,0:T(8,128)(2,1)}, bf16[32,128,1024]{2,1,0:T(8,128)(2,1)}, u32[]{:S(2)}, u32[]{:S(2)}) %collective-permute-start.3) | collective-permute-done | bytes 8388640 | tf_op jit(solution)/shard_map/ppermute | solution.py:638
  54.0 25.7 %own_tiles.1 = (f32[32,128]{1,0:T(8,128)}, f32[4,32,128,128]{3,2,1,0:T(8,128)}, f32[176,136,128]{2,1,0:T(8,128)}, f32[48,136,128]{2,1,0:T(8,128)}, f32[8,128]{1,0:T(8,128)}) custom-call(s32[28]{0:T(128)} %pad_add_fusion.2.info.refs_0_, s32[132]{0:T(256)S(1)} %copy-done.14, s32[260]{0:T(512)} %pad.9.work.refs_2_, f32[32,128]{1,0:T(8,128)} %bitcast.28, ...), custom_call_target="tpu_custom_call" | custom-call | flops 9999999827968 | bytes 30000001024 | tf_op jit(solution)/shard_map/own_tiles/pallas_call | solution.py:380
  79.7 1.9 collective-permute-start.6
  81.6 1.9 collective-permute-start.5
  83.5 2.4 feed.13
  85.9 16.0 %collective-permute-start.9 = (bf16[1024,512]{1,0:T(8,128)(2,1)}, bf16[1024,512]{1,0:T(8,128)(2,1)}, u32[]{:S(2)}, u32[]{:S(2)}) collective-permute-start(bf16[1024,512]{1,0:T(8,128)(2,1)} %get-tuple-element.117), channel_id=1, source_target_pairs={{0,1},{1,0},{2,3},{3,2},{4,5},{5,4},{6,7},{7,6},{8,9},{9,8},{10,11... | collective-permute-start | bytes 3145736 | tf_op jit(solution)/shard_map/ppermute | solution.py:652
  102.0 2.6 feed.14
  105.3 1.4 convert_element_type.56
  106.7 3.3 %collective-permute-start.16 = (f16[48,136,128]{2,1,0:T(8,128)(2,1)}, f16[48,136,128]{2,1,0:T(8,128)(2,1)}, u32[]{:S(2)}, u32[]{:S(2)}) collective-permute-start(f16[48,136,128]{2,1,0:T(8,128)(2,1)} %convert_element_type.56), channel_id=1, source_target_pairs={{0,16},{8,24},{16,0},{24,8},{1,17},{9,25},{17,1},{25,9},{2,18},{10... | collective-permute-start | bytes 5013512 | tf_op jit(solution)/shard_map/ppermute | solution.py:641
  110.0 2.3 collective-permute-start.12
  112.3 2.3 collective-permute-start.15
  114.6 10.8 %collective-permute-done.9.refs_3_ = bf16[1024,512]{1,0:T(8,128)(2,1)} collective-permute-done((bf16[1024,512]{1,0:T(8,128)(2,1)}, bf16[1024,512]{1,0:T(8,128)(2,1)}, u32[]{:S(2)}, u32[]{:S(2)}) %collective-permute-start.9) | collective-permute-done | bytes 1048608 | tf_op jit(solution)/shard_map/ppermute | solution.py:652
  125.4 5.0 %center_join.5 = (bf16[16,1024,128]{2,1,0:T(8,128)(2,1)}, f32[8,128]{1,0:T(8,128)}) custom-call(f32[32,128]{1,0:T(8,128)} %collective-permute-done.5.refs_0_, f32[32,128]{1,0:T(8,128)} %collective-permute-done.6.refs_1_, bf16[1024,512]{1,0:T(8,128)(2,1)} %collective-permute-done.7.refs_2_, bf16[1024,512]{1,0:T(8,128)(2,1)} %collective-permute-done.9.refs_3_, ...), custom_call_target="tpu_custom_call" | custom-call | flops 499999997952 | bytes 1500000000 | tf_op jit(solution)/shard_map/center_join/pallas_call | solution.py:472
  130.4 2.7 collective-permute-done.12.far.refs_5_
  133.1 2.4 feed.15
  135.9 3.3 %convert_element_type.57.refs_1_.refs_8_ = f32[48,136,128]{2,1,0:T(8,128)} convert(f16[48,136,128]{2,1,0:T(8,128)(2,1)} %collective-permute-done.16) | non-fusion elementwise | flops 835584 | bytes 5013504 | tf_op jit(solution)/shard_map/convert_element_type | solution.py:644
  139.2 5.4 %collective-permute-start.18 = (bf16[1024,512]{1,0:T(8,128)(2,1)}, bf16[1024,512]{1,0:T(8,128)(2,1)}, u32[]{:S(2)}, u32[]{:S(2)}) collective-permute-start(bf16[1024,512]{1,0:T(8,128)(2,1)} %get-tuple-element.137), channel_id=1, source_target_pairs={{2,0},{3,1},{4,2},{5,3},{6,4},{7,5},{10,8},{11,9},{12,10},{13,11},... | collective-permute-start | bytes 3145736 | tf_op jit(solution)/shard_map/ppermute | solution.py:649
  144.6 16.2 %halo_tiles.5 = (f32[4,32,128,128]{3,2,1,0:T(8,128)}, f32[176,136,128]{2,1,0:T(8,128)}, f32[8,128]{1,0:T(8,128)}, s32[1]{0:T(128)}, f32[32,136,128]{2,1,0:T(8,128)}) custom-call(s32[28]{0:T(128)} %pad_add_fusion.2.info.refs_0_, s32[132]{0:T(256)S(1)} %copy-done.15, s32[260]{0:T(512)} %pad.9.work.refs_2_, ...), custom_call_target="tpu_custom_call", output_to_operand_aliasing={{0}: (8, {}), {1}: (9, {})} | custom-call | flops 9999999827968 | bytes 30000001024 | tf_op jit(solution)/shard_map/halo_tiles/pallas_call | solution.py:553
  160.8 2.8 convert_element_type.58
  164.0 2.4 feed.16
  166.5 7.2 %collective-permute-start.21 = (bf16[1024,512]{1,0:T(8,128)(2,1)}, bf16[1024,512]{1,0:T(8,128)(2,1)}, u32[]{:S(2)}, u32[]{:S(2)}) collective-permute-start(bf16[1024,512]{1,0:T(8,128)(2,1)} %get-tuple-element.143), channel_id=1, source_target_pairs={{2,0},{3,1},{4,2},{5,3},{6,4},{7,5},{10,8},{11,9},{12,10},{13,11},... | collective-permute-start | bytes 3145736 | tf_op jit(solution)/shard_map/ppermute | solution.py:649
  173.8 5.0 %center_join.6 = (bf16[16,1024,128]{2,1,0:T(8,128)(2,1)}, f32[8,128]{1,0:T(8,128)}) custom-call(f32[32,128]{1,0:T(8,128)} %collective-permute-done.5.refs_0_, f32[32,128]{1,0:T(8,128)} %collective-permute-done.6.refs_1_, bf16[1024,512]{1,0:T(8,128)(2,1)} %collective-permute-done.13.refs_2_, bf16[1024,512]{1,0:T(8,128)(2,1)} %collective-permute-done.14.refs_3_, ...), custom_call_target="tpu_custom_call" | custom-call | flops 499999997952 | bytes 1500000000 | tf_op jit(solution)/shard_map/center_join/pallas_call | solution.py:472
  178.8 2.5 feed.17
  181.4 2.1 collective-permute-start.20
  183.4 1.5 collective-permute-done.22
  184.9 2.8 convert_element_type.59.refs_1_.refs_8_
  187.7 2.3 collective-permute-start.24
  189.9 19.3 %halo_tiles.6 = (f32[4,32,128,128]{3,2,1,0:T(8,128)}, f32[176,136,128]{2,1,0:T(8,128)}, f32[8,128]{1,0:T(8,128)}, s32[1]{0:T(128)}, f32[32,136,128]{2,1,0:T(8,128)}) custom-call(s32[28]{0:T(128)} %pad_add_fusion.2.info.refs_0_, s32[132]{0:T(256)S(1)} %copy-done.16, s32[260]{0:T(512)} %pad.9.work.refs_2_, ...), custom_call_target="tpu_custom_call", output_to_operand_aliasing={{0}: (9, {}), {1}: (10, {})} | custom-call | flops 9999999827968 | bytes 30000001024 | tf_op jit(solution)/shard_map/halo_tiles/pallas_call | solution.py:553
  209.2 2.1 feed.18
  211.5 1.1 convert_element_type.60
  212.6 5.0 %center_join.7 = (bf16[16,1024,128]{2,1,0:T(8,128)(2,1)}, f32[8,128]{1,0:T(8,128)}) custom-call(f32[32,128]{1,0:T(8,128)} %collective-permute-done.5.refs_0_, f32[32,128]{1,0:T(8,128)} %collective-permute-done.6.refs_1_, bf16[1024,512]{1,0:T(8,128)(2,1)} %collective-permute-done.19.refs_2_, bf16[1024,512]{1,0:T(8,128)(2,1)} %collective-permute-done.20.refs_3_, ...), custom_call_target="tpu_custom_call" | custom-call | flops 499999997952 | bytes 1500000000 | tf_op jit(solution)/shard_map/center_join/pallas_call | solution.py:472
  217.7 2.0 feed.19
  219.7 5.5 %collective-permute-done.23.refs_7_ = bf16[16,1024,128]{2,1,0:T(8,128)(2,1)} collective-permute-done((bf16[16,1024,128]{2,1,0:T(8,128)(2,1)}, bf16[16,1024,128]{2,1,0:T(8,128)(2,1)}, u32[]{:S(2)}, u32[]{:S(2)}) %collective-permute-start.23) | collective-permute-done | bytes 4194336 | tf_op jit(solution)/shard_map/ppermute | solution.py:638
  225.2 17.1 %halo_tiles.7 = (f32[4,32,128,128]{3,2,1,0:T(8,128)}, f32[176,136,128]{2,1,0:T(8,128)}, f32[8,128]{1,0:T(8,128)}, s32[1]{0:T(128)}) custom-call(s32[28]{0:T(128)} %pad_add_fusion.2.info.refs_0_, s32[132]{0:T(256)S(1)} %copy-done.17, s32[260]{0:T(512)} %pad.9.work.refs_2_, ...), custom_call_target="tpu_custom_call", output_to_operand_aliasing={{0}: (9, {}), {1}: (10, {})} | custom-call | flops 9999999827968 | bytes 30000001024 | tf_op jit(solution)/shard_map/halo_tiles/pallas_call | solution.py:553
  242.3 2.8 center_join.8
  245.3 2.8 convert_element_type.61.refs_8_
  248.1 1.0 copy-done.21
  249.0 13.0 %halo_tiles.8 = (f32[4,32,128,128]{3,2,1,0:T(8,128)}, f32[176,136,128]{2,1,0:T(8,128)}, f32[8,128]{1,0:T(8,128)}, s32[1]{0:T(128)}, f32[24,136,128]{2,1,0:T(8,128)}) custom-call(s32[28]{0:T(128)} %pad_add_fusion.2.info.refs_0_, s32[132]{0:T(256)S(1)} %copy-done.18, s32[260]{0:T(512)} %pad.9.work.refs_2_, ...), custom_call_target="tpu_custom_call", output_to_operand_aliasing={{0}: (9, {}), {1}: (10, {})} | custom-call | flops 9999999827968 | bytes 30000001024 | tf_op jit(solution)/shard_map/halo_tiles/pallas_call | solution.py:553
  262.0 1.6 convert_element_type.62
  263.6 17.9 %collective-permute-done.29 = f16[24,136,128]{2,1,0:T(8,128)(2,1)S(1)} collective-permute-done((f16[24,136,128]{2,1,0:T(8,128)(2,1)S(1)}, f16[24,136,128]{2,1,0:T(8,128)(2,1)S(1)}, u32[]{:S(2)}, u32[]{:S(2)}) %collective-permute-start.29) | collective-permute-done | bytes 835616 | tf_op jit(solution)/shard_map/ppermute | solution.py:641
  281.5 1.3 convert_element_type.63.refs_3_.refs_8_
  282.8 2.8 center_join.9
  285.7 3.0 collective-permute-done.30.refs_7_
  288.7 10.2 %halo_tiles.9 = (f32[4,32,128,128]{3,2,1,0:T(8,128)}, f32[176,136,128]{2,1,0:T(8,128)}, f32[8,128]{1,0:T(8,128)}, s32[1]{0:T(128)}, f32[20,136,128]{2,1,0:T(8,128)}) custom-call(s32[28]{0:T(128)} %pad_add_fusion.2.info.refs_0_, s32[132]{0:T(256)S(1)} %copy-done.19, s32[260]{0:T(512)} %pad.9.work.refs_2_, ...), custom_call_target="tpu_custom_call", output_to_operand_aliasing={{0}: (9, {}), {1}: (10, {})} | custom-call | flops 9999999827968 | bytes 30000001024 | tf_op jit(solution)/shard_map/halo_tiles/pallas_call | solution.py:553
  299.0 1.4 convert_element_type.64
  300.4 1.1 collective-permute-start.31
  301.5 1.3 slice_reduce_fusion.span
  302.8 3.9 %collective-permute-done.32 = s32[1]{0:T(128)} collective-permute-done((s32[1]{0:T(128)}, s32[1]{0:T(128)}, u32[]{:S(2)}, u32[]{:S(2)}) %collective-permute-start.32) | collective-permute-done | bytes 36 | tf_op jit(solution)/shard_map/ppermute | solution.py:753
  307.8 7.9 %collective-permute-start.33 = (s32[1]{0:T(128)}, s32[1]{0:T(128)}, u32[]{:S(2)}, u32[]{:S(2)}) collective-permute-start(s32[1]{0:T(128)} %max.9), channel_id=1, source_target_pairs={{0,2},{1,3},{2,0},{3,1},{4,6},{5,7},{6,4},{7,5},{8,10},{9,11},{10,... | collective-permute-start | bytes 20 | tf_op jit(solution)/shard_map/ppermute | solution.py:753
  316.7 1.4 collective-permute-start.34
  318.1 3.2 collective-permute-done.34
  321.9 1.2 convert_element_type.65.arrived
  323.1 2.7 merge_tiles.2
  (123 shorter events, 10.3 us)
Async XLA Ops:
  4.7 12.7 %copy-start.12 = (s32[7]{0:T(128)S(1)}, s32[7]{0:T(128)}, u32[]{:S(2)}) copy-start(s32[7]{0:T(128)} %constant.102) | copy-start | bytes 88
  4.7 12.7 %copy-start.13 = (s32[7]{0:T(128)S(1)}, s32[7]{0:T(128)}, u32[]{:S(2)}) copy-start(s32[7]{0:T(128)} %constant.97.clone) | copy-start | bytes 88
  4.7 12.9 %copy-start.2 = (s32[32,16]{0,1:T(8,128)S(1)}, s32[32,16]{0,1:T(8,128)}, u32[]{:S(2)}) copy-start(s32[32,16]{0,1:T(8,128)} %param.7) | copy-start | bytes 6148
  4.7 12.9 %copy-start.20 = (s32[4]{0:T(128)S(1)}, s32[4]{0:T(128)}, u32[]{:S(2)}) copy-start(s32[4]{0:T(128)} %constant.96.clone) | copy-start | bytes 52
  11.6 10.6 %collective-permute-start.1 = (f32[4096]{0:T(1024)}, f32[4096]{0:T(1024)S(1)}, u32[]{:S(2)}, u32[]{:S(2)}) collective-permute-start(f32[4096]{0:T(1024)} %bitcast.29), channel_id=1, source_target_pairs={{0,8},{8,0},{16,24},{24,16},{1,9},{9,1},{17,25},{25,17},{2,10},{10... | collective-permute-start | bytes 49160 | tf_op jit(solution)/shard_map/ppermute | solution.py:638
  11.6 28.9 %collective-permute-start.4 = (bf16[1024,512]{1,0:T(8,128)(2,1)}, bf16[1024,512]{1,0:T(8,128)(2,1)}, u32[]{:S(2)}, u32[]{:S(2)}) collective-permute-start(bf16[1024,512]{1,0:T(8,128)(2,1)} %get-tuple-element.111), channel_id=1, source_target_pairs={{2,0},{3,1},{4,2},{5,3},{6,4},{7,5},{10,8},{11,9},{12,10},{13,11},... | collective-permute-start | bytes 3145736 | tf_op jit(solution)/shard_map/ppermute | solution.py:649
  15.0 68.5 %collective-permute-start.8 = (bf16[1024,512]{1,0:T(8,128)(2,1)}, bf16[1024,512]{1,0:T(8,128)(2,1)}, u32[]{:S(2)}, u32[]{:S(2)}) collective-permute-start(bf16[1024,512]{1,0:T(8,128)(2,1)} %get-tuple-element.115), channel_id=1, source_target_pairs={{2,0},{3,1},{4,2},{5,3},{6,4},{7,5},{10,8},{11,9},{12,10},{13,11},... | collective-permute-start | bytes 3145736 | tf_op jit(solution)/shard_map/ppermute | solution.py:649
  21.9 5.4 %copy-start.3 = (s32[7]{0:T(128)}, s32[7]{0:T(128)S(1)}, u32[]{:S(2)}) copy-start(s32[7]{0:T(128)S(1)} %get-tuple-element.258) | copy-start | bytes 88
  21.9 5.4 %copy-start.6 = (s32[7]{0:T(128)}, s32[7]{0:T(128)S(1)}, u32[]{:S(2)}) copy-start(s32[7]{0:T(128)S(1)} %get-tuple-element.260) | copy-start | bytes 88
  22.2 18.3 %copy-start.9 = (s32[7]{0:T(128)}, s32[7]{0:T(128)S(1)}, u32[]{:S(2)}) copy-start(s32[7]{0:T(128)S(1)} %get-tuple-element.259) | copy-start | bytes 88
  22.9 3.7 %collective-permute-start.2 = (f32[4096]{0:T(1024)S(1)}, f32[4096]{0:T(1024)S(1)}, u32[]{:S(2)}, u32[]{:S(2)}) collective-permute-start(f32[4096]{0:T(1024)S(1)} %add.130), channel_id=1, source_target_pairs={{0,16},{8,24},{16,0},{24,8},{1,17},{9,25},{17,1},{25,9},{2,18},{10... | collective-permute-start | bytes 49160 | tf_op jit(solution)/shard_map/ppermute | solution.py:641
  40.5 13.5 %collective-permute-start.3 = (bf16[32,128,1024]{2,1,0:T(8,128)(2,1)}, bf16[32,128,1024]{2,1,0:T(8,128)(2,1)}, u32[]{:S(2)}, u32[]{:S(2)}) collective-permute-start(bf16[32,128,1024]{2,1,0:T(8,128)(2,1)} %center_transpose.1.xa.refs_4_), channel_id=1, source_target_pairs={{0,8},{8,0},{16,24},{24,16},{1,9},{9,1},{17,25},{25,17},{2,10},{10... | collective-permute-start | bytes 25165832 | tf_op jit(solution)/shard_map/ppermute | solution.py:638
  40.6 13.5 %copy-start.14 = (s32[132]{0:T(256)S(1)}, s32[132]{0:T(256)}, u32[]{:S(2)}) copy-start(s32[132]{0:T(256)} %pad.8.mlist.refs_1_) | copy-start | bytes 1588
  43.0 67.0 %collective-permute-start.7 = (bf16[1024,512]{1,0:T(8,128)(2,1)}, bf16[1024,512]{1,0:T(8,128)(2,1)}, u32[]{:S(2)}, u32[]{:S(2)}) collective-permute-start(bf16[1024,512]{1,0:T(8,128)(2,1)} %get-tuple-element.114), channel_id=1, source_target_pairs={{0,1},{1,0},{2,3},{3,2},{4,5},{5,4},{6,7},{7,6},{8,9},{9,8},{10,11... | collective-permute-start | bytes 3145736 | tf_op jit(solution)/shard_map/ppermute | solution.py:652
  44.6 57.4 %collective-permute-start.10 = (bf16[1024,512]{1,0:T(8,128)(2,1)}, bf16[1024,512]{1,0:T(8,128)(2,1)}, u32[]{:S(2)}, u32[]{:S(2)}) collective-permute-start(bf16[1024,512]{1,0:T(8,128)(2,1)} %get-tuple-element.118), channel_id=1, source_target_pairs={{2,0},{3,1},{4,2},{5,3},{6,4},{7,5},{10,8},{11,9},{12,10},{13,11},... | collective-permute-start | bytes 3145736 | tf_op jit(solution)/shard_map/ppermute | solution.py:649
  79.7 32.5 %collective-permute-start.6 = (f32[32,128]{1,0:T(8,128)}, f32[32,128]{1,0:T(8,128)}, u32[]{:S(2)}, u32[]{:S(2)}) collective-permute-start(f32[32,128]{1,0:T(8,128)} %get-tuple-element.113), channel_id=1, source_target_pairs={{2,0},{3,1},{4,2},{5,3},{6,4},{7,5},{10,8},{11,9},{12,10},{13,11},... | collective-permute-start | bytes 49160 | tf_op jit(solution)/shard_map/ppermute | solution.py:35
  81.6 30.7 %collective-permute-start.5 = (f32[32,128]{1,0:T(8,128)}, f32[32,128]{1,0:T(8,128)}, u32[]{:S(2)}, u32[]{:S(2)}) collective-permute-start(f32[32,128]{1,0:T(8,128)} %get-tuple-element.113), channel_id=1, source_target_pairs={{1,0},{2,1},{3,2},{4,3},{5,4},{6,5},{7,6},{9,8},{10,9},{11,10},{12... | collective-permute-start | bytes 49160 | tf_op jit(solution)/shard_map/ppermute | solution.py:35
  85.9 39.4 %collective-permute-start.9 = (bf16[1024,512]{1,0:T(8,128)(2,1)}, bf16[1024,512]{1,0:T(8,128)(2,1)}, u32[]{:S(2)}, u32[]{:S(2)}) collective-permute-start(bf16[1024,512]{1,0:T(8,128)(2,1)} %get-tuple-element.117), channel_id=1, source_target_pairs={{0,1},{1,0},{2,3},{3,2},{4,5},{5,4},{6,7},{7,6},{8,9},{9,8},{10,11... | collective-permute-start | bytes 3145736 | tf_op jit(solution)/shard_map/ppermute | solution.py:652
  102.0 3.3 %copy-start = (f32[48,136,128]{2,1,0:T(8,128)S(1)}, f32[48,136,128]{2,1,0:T(8,128)}, u32[]{:S(2)}) copy-start(f32[48,136,128]{2,1,0:T(8,128)} %get-tuple-element.132) | copy-start | bytes 10027012
  106.7 29.2 %collective-permute-start.16 = (f16[48,136,128]{2,1,0:T(8,128)(2,1)}, f16[48,136,128]{2,1,0:T(8,128)(2,1)}, u32[]{:S(2)}, u32[]{:S(2)}) collective-permute-start(f16[48,136,128]{2,1,0:T(8,128)(2,1)} %convert_element_type.56), channel_id=1, source_target_pairs={{0,16},{8,24},{16,0},{24,8},{1,17},{9,25},{17,1},{25,9},{2,18},{10... | collective-permute-start | bytes 5013512 | tf_op jit(solution)/shard_map/ppermute | solution.py:641
  110.0 23.1 %collective-permute-start.12 = (bf16[1024,512]{1,0:T(8,128)(2,1)}, bf16[1024,512]{1,0:T(8,128)(2,1)}, u32[]{:S(2)}, u32[]{:S(2)}) collective-permute-start(bf16[1024,512]{1,0:T(8,128)(2,1)} %get-tuple-element.124), channel_id=1, source_target_pairs={{2,0},{3,1},{4,2},{5,3},{6,4},{7,5},{10,8},{11,9},{12,10},{13,11},... | collective-permute-start | bytes 3145736 | tf_op jit(solution)/shard_map/ppermute | solution.py:649
  112.3 54.3 %collective-permute-start.13 = (bf16[1024,512]{1,0:T(8,128)(2,1)}, bf16[1024,512]{1,0:T(8,128)(2,1)}, u32[]{:S(2)}, u32[]{:S(2)}) collective-permute-start(bf16[1024,512]{1,0:T(8,128)(2,1)} %get-tuple-element.128), channel_id=1, source_target_pairs={{0,1},{1,0},{2,3},{3,2},{4,5},{5,4},{6,7},{7,6},{8,9},{9,8},{10,11... | collective-permute-start | bytes 3145736 | tf_op jit(solution)/shard_map/ppermute | solution.py:652
  112.3 51.8 %collective-permute-start.15 = (bf16[1024,512]{1,0:T(8,128)(2,1)}, bf16[1024,512]{1,0:T(8,128)(2,1)}, u32[]{:S(2)}, u32[]{:S(2)}) collective-permute-start(bf16[1024,512]{1,0:T(8,128)(2,1)} %get-tuple-element.130), channel_id=1, source_target_pairs={{2,0},{3,1},{4,2},{5,3},{6,4},{7,5},{10,8},{11,9},{12,10},{13,11},... | collective-permute-start | bytes 3145736 | tf_op jit(solution)/shard_map/ppermute | solution.py:649
  130.3 14.2 %collective-permute-start.11 = (bf16[16,1024,128]{2,1,0:T(8,128)(2,1)}, bf16[16,1024,128]{2,1,0:T(8,128)(2,1)}, u32[]{:S(2)}, u32[]{:S(2)}) collective-permute-start(bf16[16,1024,128]{2,1,0:T(8,128)(2,1)} %get-tuple-element.121.refs_6_), channel_id=1, source_target_pairs={{0,8},{8,0},{16,24},{24,16},{1,9},{9,1},{17,25},{25,17},{2,10},{10... | collective-permute-start | bytes 12582920 | tf_op jit(solution)/shard_map/ppermute | solution.py:638
  135.5 9.1 %copy-start.15 = (s32[132]{0:T(256)S(1)}, s32[132]{0:T(256)}, u32[]{:S(2)}) copy-start(s32[132]{0:T(256)} %pad.8.mlist.refs_1_) | copy-start | bytes 1588
  135.5 38.3 %collective-permute-start.14 = (bf16[1024,512]{1,0:T(8,128)(2,1)}, bf16[1024,512]{1,0:T(8,128)(2,1)}, u32[]{:S(2)}, u32[]{:S(2)}) collective-permute-start(bf16[1024,512]{1,0:T(8,128)(2,1)} %get-tuple-element.129), channel_id=1, source_target_pairs={{0,1},{1,0},{2,3},{3,2},{4,5},{5,4},{6,7},{7,6},{8,9},{9,8},{10,11... | collective-permute-start | bytes 3145736 | tf_op jit(solution)/shard_map/ppermute | solution.py:652
  139.2 39.6 %collective-permute-start.18 = (bf16[1024,512]{1,0:T(8,128)(2,1)}, bf16[1024,512]{1,0:T(8,128)(2,1)}, u32[]{:S(2)}, u32[]{:S(2)}) collective-permute-start(bf16[1024,512]{1,0:T(8,128)(2,1)} %get-tuple-element.137), channel_id=1, source_target_pairs={{2,0},{3,1},{4,2},{5,3},{6,4},{7,5},{10,8},{11,9},{12,10},{13,11},... | collective-permute-start | bytes 3145736 | tf_op jit(solution)/shard_map/ppermute | solution.py:649
  163.5 21.4 %collective-permute-start.22 = (f16[32,136,128]{2,1,0:T(8,128)(2,1)}, f16[32,136,128]{2,1,0:T(8,128)(2,1)}, u32[]{:S(2)}, u32[]{:S(2)}) collective-permute-start(f16[32,136,128]{2,1,0:T(8,128)(2,1)} %convert_element_type.58), channel_id=1, source_target_pairs={{0,16},{8,24},{16,0},{24,8},{1,17},{9,25},{17,1},{25,9},{2,18},{10... | collective-permute-start | bytes 3342344 | tf_op jit(solution)/shard_map/ppermute | solution.py:641
  166.4 46.2 %collective-permute-start.19 = (bf16[1024,512]{1,0:T(8,128)(2,1)}, bf16[1024,512]{1,0:T(8,128)(2,1)}, u32[]{:S(2)}, u32[]{:S(2)}) collective-permute-start(bf16[1024,512]{1,0:T(8,128)(2,1)} %get-tuple-element.141), channel_id=1, source_target_pairs={{0,1},{1,0},{2,3},{3,2},{4,5},{5,4},{6,7},{7,6},{8,9},{9,8},{10,11... | collective-permute-start | bytes 3145736 | tf_op jit(solution)/shard_map/ppermute | solution.py:652
  166.5 42.7 %collective-permute-start.21 = (bf16[1024,512]{1,0:T(8,128)(2,1)}, bf16[1024,512]{1,0:T(8,128)(2,1)}, u32[]{:S(2)}, u32[]{:S(2)}) collective-permute-start(bf16[1024,512]{1,0:T(8,128)(2,1)} %get-tuple-element.143), channel_id=1, source_target_pairs={{2,0},{3,1},{4,2},{5,3},{6,4},{7,5},{10,8},{11,9},{12,10},{13,11},... | collective-permute-start | bytes 3145736 | tf_op jit(solution)/shard_map/ppermute | solution.py:649
  178.7 11.2 %collective-permute-start.17 = (bf16[16,1024,128]{2,1,0:T(8,128)(2,1)}, bf16[16,1024,128]{2,1,0:T(8,128)(2,1)}, u32[]{:S(2)}, u32[]{:S(2)}) collective-permute-start(bf16[16,1024,128]{2,1,0:T(8,128)(2,1)} %get-tuple-element.134.refs_6_), channel_id=1, source_target_pairs={{0,8},{8,0},{16,24},{24,16},{1,9},{9,1},{17,25},{25,17},{2,10},{10... | collective-permute-start | bytes 12582920 | tf_op jit(solution)/shard_map/ppermute | solution.py:638
  178.8 11.1 %copy-start.16 = (s32[132]{0:T(256)S(1)}, s32[132]{0:T(256)}, u32[]{:S(2)}) copy-start(s32[132]{0:T(256)} %pad.8.mlist.refs_1_) | copy-start | bytes 1588
  181.4 31.3 %collective-permute-start.20 = (bf16[1024,512]{1,0:T(8,128)(2,1)}, bf16[1024,512]{1,0:T(8,128)(2,1)}, u32[]{:S(2)}, u32[]{:S(2)}) collective-permute-start(bf16[1024,512]{1,0:T(8,128)(2,1)} %get-tuple-element.142), channel_id=1, source_target_pairs={{0,1},{1,0},{2,3},{3,2},{4,5},{5,4},{6,7},{7,6},{8,9},{9,8},{10,11... | collective-permute-start | bytes 3145736 | tf_op jit(solution)/shard_map/ppermute | solution.py:652
  187.7 30.0 %collective-permute-start.24 = (bf16[1024,512]{1,0:T(8,128)(2,1)}, bf16[1024,512]{1,0:T(8,128)(2,1)}, u32[]{:S(2)}, u32[]{:S(2)}) collective-permute-start(bf16[1024,512]{1,0:T(8,128)(2,1)} %get-tuple-element.150), channel_id=1, source_target_pairs={{2,0},{3,1},{4,2},{5,3},{6,4},{7,5},{10,8},{11,9},{12,10},{13,11},... | collective-permute-start | bytes 3145736 | tf_op jit(solution)/shard_map/ppermute | solution.py:649
  209.2 2.2 copy-start.1
  211.4 30.9 %collective-permute-start.25 = (bf16[1024,512]{1,0:T(8,128)(2,1)}, bf16[1024,512]{1,0:T(8,128)(2,1)}, u32[]{:S(2)}, u32[]{:S(2)}) collective-permute-start(bf16[1024,512]{1,0:T(8,128)(2,1)} %get-tuple-element.154), channel_id=1, source_target_pairs={{0,1},{1,0},{2,3},{3,2},{4,5},{5,4},{6,7},{7,6},{8,9},{9,8},{10,11... | collective-permute-start | bytes 3145736 | tf_op jit(solution)/shard_map/ppermute | solution.py:652
  212.6 32.7 %collective-permute-start.27 = (f16[32,136,128]{2,1,0:T(8,128)(2,1)}, f16[32,136,128]{2,1,0:T(8,128)(2,1)}, u32[]{:S(2)}, u32[]{:S(2)}) collective-permute-start(f16[32,136,128]{2,1,0:T(8,128)(2,1)} %convert_element_type.60), channel_id=1, source_target_pairs={{0,16},{8,24},{16,0},{24,8},{1,17},{9,25},{17,1},{25,9},{2,18},{10... | collective-permute-start | bytes 3342344 | tf_op jit(solution)/shard_map/ppermute | solution.py:641
  217.6 7.6 %collective-permute-start.23 = (bf16[16,1024,128]{2,1,0:T(8,128)(2,1)}, bf16[16,1024,128]{2,1,0:T(8,128)(2,1)}, u32[]{:S(2)}, u32[]{:S(2)}) collective-permute-start(bf16[16,1024,128]{2,1,0:T(8,128)(2,1)} %get-tuple-element.147.refs_6_), channel_id=1, source_target_pairs={{0,8},{8,0},{16,24},{24,16},{1,9},{9,1},{17,25},{25,17},{2,10},{10... | collective-permute-start | bytes 12582920 | tf_op jit(solution)/shard_map/ppermute | solution.py:638
  217.7 7.5 %copy-start.17 = (s32[132]{0:T(256)S(1)}, s32[132]{0:T(256)}, u32[]{:S(2)}) copy-start(s32[132]{0:T(256)} %pad.8.mlist.refs_1_) | copy-start | bytes 1588
  242.3 6.7 %copy-start.18 = (s32[132]{0:T(256)S(1)}, s32[132]{0:T(256)}, u32[]{:S(2)}) copy-start(s32[132]{0:T(256)} %pad.8.mlist.refs_1_) | copy-start | bytes 1588
  245.1 2.9 collective-permute-start.26
  245.2 37.6 %collective-permute-start.28 = (bf16[1024,512]{1,0:T(8,128)(2,1)}, bf16[1024,512]{1,0:T(8,128)(2,1)}, u32[]{:S(2)}, u32[]{:S(2)}) collective-permute-start(bf16[1024,512]{1,0:T(8,128)(2,1)} %get-tuple-element.162), channel_id=1, source_target_pairs={{0,1},{1,0},{2,3},{3,2},{4,5},{5,4},{6,7},{7,6},{8,9},{9,8},{10,11... | collective-permute-start | bytes 3145736 | tf_op jit(solution)/shard_map/ppermute | solution.py:652
  248.1 1.0 copy-start.21
  263.6 18.0 %collective-permute-start.29 = (f16[24,136,128]{2,1,0:T(8,128)(2,1)S(1)}, f16[24,136,128]{2,1,0:T(8,128)(2,1)S(1)}, u32[]{:S(2)}, u32[]{:S(2)}) collective-permute-start(f16[24,136,128]{2,1,0:T(8,128)(2,1)S(1)} %convert_element_type.62), channel_id=1, source_target_pairs={{0,16},{8,24},{16,0},{24,8},{1,17},{9,25},{17,1},{25,9},{2,18},{10... | collective-permute-start | bytes 2506760 | tf_op jit(solution)/shard_map/ppermute | solution.py:641
  285.6 3.1 collective-permute-start.30
  285.7 3.0 copy-start.19
  300.4 21.5 %collective-permute-start.31 = (f16[20,136,128]{2,1,0:T(8,128)(2,1)S(1)}, f16[20,136,128]{2,1,0:T(8,128)(2,1)S(1)}, u32[]{:S(2)}, u32[]{:S(2)}) collective-permute-start(f16[20,136,128]{2,1,0:T(8,128)(2,1)S(1)} %convert_element_type.64), channel_id=1, source_target_pairs={{0,16},{8,24},{16,0},{24,8},{1,17},{9,25},{17,1},{25,9},{2,18},{10... | collective-permute-start | bytes 2088968 | tf_op jit(solution)/shard_map/ppermute | solution.py:641
  302.8 3.9 %collective-permute-start.32 = (s32[1]{0:T(128)}, s32[1]{0:T(128)}, u32[]{:S(2)}, u32[]{:S(2)}) collective-permute-start(s32[1]{0:T(128)} %get-tuple-element.171), channel_id=1, source_target_pairs={{0,1},{1,0},{2,3},{3,2},{4,5},{5,4},{6,7},{7,6},{8,9},{9,8},{10,11... | collective-permute-start | bytes 20 | tf_op jit(solution)/shard_map/ppermute | solution.py:753
  307.8 8.3 %collective-permute-start.33 = (s32[1]{0:T(128)}, s32[1]{0:T(128)}, u32[]{:S(2)}, u32[]{:S(2)}) collective-permute-start(s32[1]{0:T(128)} %max.9), channel_id=1, source_target_pairs={{0,2},{1,3},{2,0},{3,1},{4,6},{5,7},{6,4},{7,5},{8,10},{9,11},{10,... | collective-permute-start | bytes 20 | tf_op jit(solution)/shard_map/ppermute | solution.py:753
  316.7 4.6 %collective-permute-start.34 = (s32[1]{0:T(128)}, s32[1]{0:T(128)}, u32[]{:S(2)}, u32[]{:S(2)}) collective-permute-start(s32[1]{0:T(128)} %max.10), channel_id=1, source_target_pairs={{0,4},{1,5},{2,6},{3,7},{4,0},{5,1},{6,2},{7,3},{8,12},{9,13},{10,... | collective-permute-start | bytes 20 | tf_op jit(solution)/shard_map/ppermute | solution.py:753
  323.1 2.7 copy-start.4
  323.1 2.7 copy-start.7
  323.1 2.7 copy-start.10
